TPU v7x, 512 devices: a whole 4x4x16 slice. The times are simulated.
512 devices in a mesh: layer: 16 (over x_hi, y, core), plane: 32 (over x_lo, z).
Axes of the slice: x: 4 (x_hi: 2, x_lo: 2; x = x_hi * 2 + x_lo), y: 4, z: 16, core: 2. Of those that a mesh axis runs over, the one named last changes fastest.
Arguments:
- polar: float32 [16, 512, 512], P('layer', 'plane'), may hold values from 0.1 to 1.6
- azimuth: float32 [16, 512, 512], P('layer', 'plane'), may hold values from -3 to 3
- saturation: float32 [16, 512, 512], P('layer', 'plane'), may hold values from 0.5 to 1.5
- anisotropy: float32 [16, 512, 512], P('layer', 'plane'), may hold values from 0.3 to 1.5
- stiffness: float32 [16], P('layer'), may hold values from 0.35 to 0.7
- coupling: float32 [15], replicated, may hold values from -1 to 1
Outputs:
- field: float32 [16, 3, 512, 512], P('layer', None, 'plane')
- moment: float32 [16, 3, 512, 512], P('layer', None, 'plane')
All inputs are finite; a program needn't handle non-finite values.
Results may differ from a plain program's by a relative error of at most 0.00005.
Values sent between devices are 32-bit elements; how exact they have to be, the bound alone decides.
A program may use at most 64 MiB of HBM per device.

v0:
```python
import functools
import math

import jax
import jax.numpy as jnp
import ml_dtypes
import numpy as np
from jax import lax
from jax.experimental import pallas as pl
from jax.experimental.pallas import tpu as pltpu
from jax.sharding import PartitionSpec as P

side_length = 512.0
spacing = 1.2
damping = 0.1
time_step = 0.1

CELLS = 512
PAD = 2 * CELLS
LAYERS = 16
RING = 16
SLAB = 32
MESH = pl.DeviceIdType.MESH
f32 = jnp.float32
bf16 = jnp.bfloat16


def halves(table):
    high = table.astype(ml_dtypes.bfloat16)
    low = (table - high.astype(np.float64)).astype(ml_dtypes.bfloat16)
    return high, low


@functools.lru_cache(None)
def transforms():
    column = np.arange(PAD)
    pair, part = column // 128, column // 64 % 2
    wave = (2 * pair + column % 2) * SLAB + column // 2 % SLAB
    place = np.arange(CELLS)
    angle = (place[:, None] * wave[None, :] % PAD) * (2.0 * np.pi / PAD)
    along_y = np.where(part[None, :] == 0, np.cos(angle), np.sin(angle))
    alternating = np.where(place % 2 == 0, 1.0, -1.0)
    along_y[:, (wave == 0) & (part == 1)] = alternating[:, None]
    row = np.arange(CELLS)
    x = row // 256 * 256 + row // 8 % 16 * 16 + row // 128 % 2 * 8 + row % 8
    angle = (x[:, None] * np.arange(CELLS)[None, :] % PAD) * (2.0 * np.pi / PAD)
    sine = np.sin(angle)
    sine[:, 0] = np.where(x % 2 == 0, 1.0, -1.0)
    along_x = np.concatenate([np.cos(angle), sine], 1)
    return halves(along_y) + halves(along_x)


def polynomial(x, coefficients):
    total = jnp.full_like(x, coefficients[-1])
    for c in coefficients[-2::-1]:
        total = total * x + c
    return total


SIN = [(-1.0) ** n / math.factorial(2 * n + 1) for n in range(7)]
COS = [(-1.0) ** n / math.factorial(2 * n) for n in range(8)]
SINH = [1.0 / math.factorial(2 * n + 1) for n in range(11)]


def sin_cos(x):
    square = x * x
    return x * polynomial(square, SIN), polynomial(square, COS)


def unit_moment(polar, azimuth):
    sin_p, cos_p = sin_cos(polar)
    s, c = sin_cos(0.5 * azimuth)
    return sin_p * (1.0 - 2.0 * s * s), sin_p * (2.0 * s * c), cos_p


def product(left, high_ref, low_ref, transposed):
    high = left.astype(bf16)
    low = (left - high.astype(f32)).astype(bf16)
    rows = left.shape[0]
    dims = (((1,), (1 if transposed else 0,)), ((), ()))
    both = lax.dot_general(
        jnp.concatenate([high, low], 0), high_ref[...], dims, preferred_element_type=f32
    )
    rest = lax.dot_general(high, low_ref[...], dims, preferred_element_type=f32)
    return both[:rows] + both[rows:] + rest


def even_lanes():
    return lax.broadcasted_iota(jnp.int32, (8, 128), 1) % 2 == 0


def forward_y(m, saturation, wyh, wyl, s1):
    rows = [m[c][8 * h : 8 * h + 8] * saturation[8 * h : 8 * h + 8] for h in range(2) for c in range(3)]
    y = product(jnp.concatenate(rows, 0), wyh, wyl, False)
    even = even_lanes()
    for c in range(3):
        for p in range(8):
            upper = y[8 * c : 8 * c + 8, 128 * p : 128 * p + 128]
            lower = y[24 + 8 * c : 32 + 8 * c, 128 * p : 128 * p + 128]
            s1[2 * p, c] = jnp.where(even, upper, pltpu.roll(lower, 1, 1))
            s1[2 * p + 1, c] = jnp.where(even, pltpu.roll(upper, 127, 1), lower)


def turn_in(r1, s2):
    for c in range(3):
        block = r1[:, c].reshape(128, 128).T
        for b in range(2):
            s2[pl.ds(2 * c + b, 64, stride=8), :] = block[64 * b : 64 * b + 64]


def spectral_tables(fy, tb):
    sub = lax.broadcasted_iota(jnp.int32, (8, 128), 0)
    fx = sub % 4 * 128 + lax.broadcasted_iota(jnp.int32, (8, 128), 1)
    second = sub // 4 == 1
    sign = jnp.where(second, 1.0, -1.0)
    edge_x = fx == 0
    edge_y = jnp.full((8, 128), fy) == 0
    for v in range(2):
        sine_y = second if v == 0 else jnp.logical_not(second)
        high_x = jnp.logical_and(edge_x, second)
        high_y = jnp.logical_and(edge_y, sine_y)
        wave_x = jnp.where(high_x, CELLS, fx).astype(f32) * (math.pi / side_length)
        wave_y = jnp.where(high_y, CELLS, fy).astype(f32) * (math.pi / side_length)
        k = jnp.sqrt(wave_x * wave_x + wave_y * wave_y)
        nonzero = k > 0.0
        safe = jnp.where(nonzero, k, 1.0)
        inverse = 1.0 / safe
        half = 0.5 * safe
        ratio = polynomial(half * half, SINH)
        self_part = jnp.where(nonzero, jnp.exp(-half) * ratio, 1.0)
        mutual = jnp.where(nonzero, half * ratio * ratio, 0.0)
        weight = jnp.where(edge_x, 1.0, 2.0) * jnp.where(edge_y, 1.0, 2.0) * (1.0 / (PAD * PAD))
        ux, uy = wave_x * inverse, wave_y * inverse
        tb[v, 0] = jnp.exp(-spacing * k)
        tb[v, 1] = weight * (1.0 - self_part)
        tb[v, 2] = weight * mutual
        tb[v, 3] = weight * self_part
        tb[v, 4] = jnp.where(edge_x, 0.0, sign * ux)
        tb[v, 5] = jnp.where(edge_y, 0.0, sign * uy)
        tb[v, 6] = jnp.where(high_x, ux, 0.0)
        tb[v, 7] = jnp.where(high_y, uy, 0.0)


ORDER = [(0, 0), (1, 1), (0, 1), (1, 0)]
ORDER_X = [(1, 1), (0, 0), (1, 0), (0, 1)]


def tile_row(c, tg, cls, lb):
    return ((c * 2 + tg) * 16 + cls * 4 + lb) * 8


def transform_x(r2, wxh, wxl, zs):
    columns = []
    for x_lo in range(2):
        for h in range(2):
            parts = [r2[pl.ds(x_lo * 16 + h * 8 + q, 16, stride=32), :] for q in range(6)]
            columns.append(jnp.concatenate(parts, 0))
    z = product(jnp.concatenate(columns, 1), wxh, wxl, False)
    for c in range(3):
        for cls, (a, b) in enumerate(ORDER_X if c == 0 else ORDER):
            for tg in range(2):
                for lb in range(4):
                    row = (2 * c + b) * 16 + tg * 8
                    lane = a * 512 + lb * 128
                    zs[pl.ds(tile_row(c, tg, cls, lb), 8), :] = z[row : row + 8, lane : lane + 128]


def couple(zs, tb, ws):
    def at(c, t, v):
        return pl.ds(tile_row(c, t // 8, 2 * v, 0) + t % 8, 8, stride=8)

    for v in range(2):
        other = 1 - v
        decay, direct, mutual = tb[v, 0], tb[v, 1], tb[v, 2]
        ux, uy, lone_x, lone_y = tb[v, 4], tb[v, 5], tb[v, 6], tb[v, 7]
        if v == 1:
            uy = -uy
        carry = jnp.zeros((8, 128), f32)
        carry_lone = jnp.zeros((8, 128), f32)
        for t in range(LAYERS):
            r = ux * zs[at(0, t, other), :] + uy * zs[at(1, t, other), :]
            lone = lone_x * pltpu.roll(zs[at(0, t, v), :], 4, 0) + lone_y * zs[at(1, t, v), :]
            ws[v, t, 0] = r
            ws[v, t, 1] = lone
            ws[v, t, 2] = carry
            ws[v, t, 3] = carry_lone
            carry = decay * (carry + (zs[at(2, t, v), :] + r))
            carry_lone = decay * (carry_lone + lone)
    for v in range(2):
        decay, direct, mutual = tb[v, 0], tb[v, 1], tb[v, 2]
        carry = jnp.zeros((8, 128), f32)
        carry_lone = jnp.zeros((8, 128), f32)
        for t in range(LAYERS - 1, -1, -1):
            r, lone = ws[v, t, 0], ws[v, t, 1]
            below, below_lone = ws[v, t, 2], ws[v, t, 3]
            z = zs[at(2, t, v), :]
            ws[v, t, 0] = direct * r + mutual * (below + carry)
            ws[v, t, 1] = direct * lone + mutual * (below_lone + carry_lone)
            zs[at(2, t, v), :] = mutual * (below - carry) - tb[v, 3] * z
            carry = decay * (carry + (r - z))
            carry_lone = decay * (carry_lone + lone)
    for v in range(2):
        other = 1 - v
        ux, uy, lone_x, lone_y = tb[other, 4], tb[v, 5], tb[v, 6], tb[v, 7]
        if v == 1:
            uy = -uy
        for t in range(LAYERS):
            h, lone = ws[other, t, 0], ws[v, t, 1]
            zs[at(0, t, v), :] = -ux * h - pltpu.roll(lone_x * lone, 4, 0)
            zs[at(1, t, v), :] = uy * h - lone_y * lone


def return_x(zs, wxh, wxl, s3):
    rows = []
    for c in range(3):
        order = ORDER_X if c == 0 else ORDER
        for b in range(2):
            for tg in range(2):
                lanes = [
                    zs[pl.ds(tile_row(c, tg, order.index((a, b)), lb), 8), :] for a in range(2) for lb in range(4)
                ]
                rows.append(jnp.concatenate(lanes, 1))
    out = product(jnp.concatenate(rows, 0), wxh, wxl, True)
    for x_lo in range(2):
        for h in range(2):
            lane = (x_lo * 2 + h) * 128
            for q in range(6):
                s3[pl.ds(x_lo * 16 + h * 8 + q, 16, stride=32), :] = out[16 * q : 16 * q + 16, lane : lane + 128]


def turn_out(r3, s4):
    for c in range(3):
        parts = [r3[pl.ds(2 * c + b, 64, stride=8), :] for b in range(2)]
        s4[:, c] = jnp.concatenate(parts, 0).T.reshape(16, 8, 128)


def inverse_y(r4, wyh, wyl):
    even = even_lanes()
    upper, lower = [], []
    for c in range(3):
        up, low = [], []
        for p in range(8):
            first, second = r4[2 * p, c], r4[2 * p + 1, c]
            up.append(jnp.where(even, first, pltpu.roll(second, 1, 1)))
            low.append(jnp.where(even, pltpu.roll(first, 127, 1), second))
        upper.append(jnp.concatenate(up, 1))
        lower.append(jnp.concatenate(low, 1))
    out = product(jnp.concatenate(upper + lower, 0), wyh, wyl, True)
    return [jnp.concatenate([out[8 * c : 8 * c + 8], out[24 + 8 * c : 32 + 8 * c]], 0) for c in range(3)]


def cross_product(a, b):
    return (a[1] * b[2] - a[2] * b[1], a[2] * b[0] - a[0] * b[2], a[0] * b[1] - a[1] * b[0])


def other_fields(m, first_row, last_row, lower_m, upper_m, stiffness, lower_link, upper_link, anisotropy):
    lane = lax.broadcasted_iota(jnp.int32, (16, 512), 1)
    fields = []
    for c in range(3):
        beside = jnp.concatenate([first_row[c], m[c][:15]], 0) + jnp.concatenate([m[c][1:], last_row[c]], 0)
        beside = beside + jnp.where(lane == 0, 0.0, pltpu.roll(m[c], 1, 1))
        beside = beside + jnp.where(lane == 511, 0.0, pltpu.roll(m[c], 511, 1))
        fields.append(stiffness * beside + lower_link * lower_m[c] + upper_link * upper_m[c])
    fields[2] = fields[2] + anisotropy * m[2]
    return fields


def step(m, field):
    first = cross_product(m, field)
    second = cross_product(m, first)
    scale = -time_step / (1.0 + damping * damping)
    stepped = [m[c] + scale * (first[c] + damping * second[c]) for c in range(3)]
    inverse = lax.rsqrt(stepped[0] * stepped[0] + stepped[1] * stepped[1] + stepped[2] * stepped[2])
    return [s * inverse for s in stepped]


def kernel(
    polar, azimuth, saturation, anisotropy, stiffness, coupling, wyh_any, wyl_any, wxh_any, wxl_any,
    field_out, moment_out,
    wyh, wyl, wxh, wxl, s1, r1, s2, r2, s3, r3, s4, r4, zs, ws, tb, near, edge_out, edge_in, rest,
    load_sem, send_sem, recv_sem, near_send, near_recv, edge_send, edge_recv,
):
    t = lax.axis_index("layer")
    p = lax.axis_index("plane")
    z = lax.rem(p, RING)
    x_lo = lax.div(p, RING)
    f = t * 2 + x_lo

    loads = [
        pltpu.make_async_copy(src, dst, load_sem.at[i])
        for i, (src, dst) in enumerate([(wyh_any, wyh), (wyl_any, wyl), (wxh_any, wxh), (wxl_any, wxl)])
    ]
    for load in loads:
        load.start()

    def ring_device(i):
        dist = RING // 2 - lax.div(i + 1, 2)
        there = lax.rem(z + jnp.where(lax.rem(i, 2) == 1, dist, RING - dist), RING)
        return there, (t, x_lo * RING + there)

    def slab_device(i):
        there = lax.rem(f + 1 + i, SLAB)
        return there, (lax.div(there, 2), lax.rem(there, 2) * RING + z)

    next_plane = (t, lax.rem(p + 1, 2 * RING))
    last_plane = (t, lax.rem(p + 2 * RING - 1, 2 * RING))
    next_layer = (lax.rem(t + 1, LAYERS), p)
    last_layer = (lax.rem(t + LAYERS - 1, LAYERS), p)

    barrier = pltpu.get_barrier_semaphore()

    def greet(where):
        def one(i, carry):
            pl.semaphore_signal(barrier, inc=1, device_id=where(i)[1], device_id_type=MESH)
            return carry

        return one

    lax.fori_loop(0, RING - 1, greet(ring_device), 0)
    lax.fori_loop(0, SLAB - 1, greet(slab_device), 0)
    for there in (next_plane, last_plane):
        pl.semaphore_signal(barrier, inc=1, device_id=there, device_id_type=MESH)

    m = unit_moment(polar[0], azimuth[0])
    edge_out[...] = jnp.zeros((2, 16, 128), f32)
    for side, row in enumerate((0, 15)):
        for c in range(3):
            for lb in range(4):
                edge_out[side, c * 4 + lb : c * 4 + lb + 1, :] = m[c][row : row + 1, 128 * lb : 128 * lb + 128]
    s2[...] = jnp.zeros((512, 128), f32)
    s3[...] = jnp.zeros((512, 128), f32)
    loads[0].wait()
    loads[1].wait()
    forward_y(m, saturation[0], wyh, wyl, s1)

    pl.semaphore_wait(barrier, RING - 1 + SLAB - 1 + 2)

    def remote(src, dst, sem, there):
        return pltpu.make_async_remote_copy(
            src_ref=src, dst_ref=dst, send_sem=sem[0], recv_sem=sem[1], device_id=there, device_id_type=MESH
        )

    def ring_send(src, dst, n):
        def one(i, carry):
            there, device = ring_device(i)
            remote(src.at[there], dst.at[z], (send_sem.at[n], recv_sem.at[n]), device).start()
            return carry

        lax.fori_loop(0, RING - 1, one, 0)
        pltpu.make_async_copy(src.at[z], dst.at[z], recv_sem.at[n]).start()

    def rows_of(ref, i):
        return ref.at[pl.ds(pl.multiple_of(i * 16, 16), 16)]

    def slab_send(src, dst, n):
        def one(i, carry):
            there, device = slab_device(i)
            remote(rows_of(src, there), rows_of(dst, f), (send_sem.at[n], recv_sem.at[n]), device).start()
            return carry

        lax.fori_loop(0, SLAB - 1, one, 0)
        pltpu.make_async_copy(rows_of(src, f), rows_of(dst, f), recv_sem.at[n]).start()

    def received(dst, n):
        pltpu.make_async_copy(dst, dst, recv_sem.at[n]).wait()

    ring_send(s1, r1, 0)
    sides = []
    for i, (ref, side, there) in enumerate(
        [(polar, 0, next_layer), (azimuth, 0, next_layer), (polar, 1, last_layer), (azimuth, 1, last_layer)]
    ):
        sides.append(remote(ref.at[0], near.at[side, i % 2], (near_send.at[i], near_recv.at[i]), there))
    for side, there in ((0, last_plane), (1, next_plane)):
        sides.append(
            remote(edge_out.at[side], edge_in.at[1 - side], (edge_send.at[side], edge_recv.at[side]), there)
        )
    for copy in sides:
        copy.start()

    spectral_tables(z * SLAB + f, tb)
    for copy in sides:
        copy.wait_recv()
    lower_m = unit_moment(near[0, 0], near[0, 1])
    upper_m = unit_moment(near[1, 0], near[1, 1])
    lower_link = jnp.where(t > 0, coupling[jnp.maximum(t - 1, 0)], 0.0)
    upper_link = jnp.where(t < LAYERS - 1, coupling[jnp.minimum(t, LAYERS - 2)], 0.0)

    def edge_row(side, present):
        rows = []
        for c in range(3):
            lanes = [edge_in[side, c * 4 + lb : c * 4 + lb + 1, :] for lb in range(4)]
            rows.append(jnp.where(present, jnp.concatenate(lanes, 1), 0.0))
        return rows

    m = unit_moment(polar[0], azimuth[0])
    fields = other_fields(
        m, edge_row(0, p > 0), edge_row(1, p < 2 * RING - 1), lower_m, upper_m,
        stiffness[0], lower_link, upper_link, anisotropy[0],
    )
    for c in range(3):
        rest[c] = fields[c]
        rest[3 + c] = m[c]

    received(r1, 0)
    turn_in(r1, s2)
    slab_send(s2, r2, 1)
    loads[2].wait()
    loads[3].wait()
    received(r2, 1)
    transform_x(r2, wxh, wxl, zs)
    couple(zs, tb, ws)
    return_x(zs, wxh, wxl, s3)
    slab_send(s3, r3, 2)
    received(r3, 2)
    turn_out(r3, s4)
    ring_send(s4, r4, 3)
    received(r4, 3)
    demag = inverse_y(r4, wyh, wyl)
    m = [rest[3 + c] for c in range(3)]
    field = [demag[c] + rest[c] for c in range(3)]
    moment = step(m, field)
    for c in range(3):
        field_out[0, c] = field[c]
        moment_out[0, c] = moment[c]

    for copy in sides:
        copy.wait_send()
    ring_part = s1.at[pl.ds(0, RING - 1)]
    slab_part = s2.at[pl.ds(0, 16 * (SLAB - 1))]
    for n, part in ((0, ring_part), (1, slab_part), (2, slab_part), (3, ring_part)):
        pltpu.make_async_copy(part, part, send_sem.at[n]).wait()


def body(polar, azimuth, saturation, anisotropy, stiffness, coupling):
    vmem = pl.BlockSpec(memory_space=pltpu.VMEM)
    smem = pl.BlockSpec(memory_space=pltpu.SMEM)
    hbm = pl.BlockSpec(memory_space=pl.ANY)
    out = jax.ShapeDtypeStruct((1, 3, 16, CELLS), f32)
    dma = pltpu.SemaphoreType.DMA
    ring = pltpu.VMEM((RING, 3, 8, 128), f32)
    slab = pltpu.VMEM((SLAB * 16, 128), f32)
    return pl.pallas_call(
        kernel,
        out_shape=(out, out),
        in_specs=[vmem] * 4 + [smem] * 2 + [hbm] * 4,
        out_specs=(vmem, vmem),
        scratch_shapes=[
            pltpu.VMEM((CELLS, PAD), bf16),
            pltpu.VMEM((CELLS, PAD), bf16),
            pltpu.VMEM((CELLS, PAD), bf16),
            pltpu.VMEM((CELLS, PAD), bf16),
            ring, ring, slab, slab, slab, slab, ring, ring,
            pltpu.VMEM((3 * 2 * 16 * 8, 128), f32),
            pltpu.VMEM((2, LAYERS, 4, 8, 128), f32),
            pltpu.VMEM((2, 8, 8, 128), f32),
            pltpu.VMEM((2, 2, 16, CELLS), f32),
            pltpu.VMEM((2, 16, 128), f32),
            pltpu.VMEM((2, 16, 128), f32),
            pltpu.VMEM((6, 16, CELLS), f32),
            dma((4,)), dma((4,)), dma((4,)), dma((4,)), dma((4,)), dma((2,)), dma((2,)),
        ],
        compiler_params=pltpu.CompilerParams(
            collective_id=0, has_side_effects=True, vmem_limit_bytes=40 * 1024 * 1024
        ),
        cost_estimate=pl.CostEstimate(flops=10**9, bytes_accessed=5 * 10**6, transcendentals=0),
        name="fields",
    )(polar, azimuth, saturation, anisotropy, stiffness, coupling, *transforms())


def solution(mesh):
    placed = (
        P("layer", "plane", None),
        P("layer", "plane", None),
        P("layer", "plane", None),
        P("layer", "plane", None),
        P("layer"),
        P(),
    )
    return jax.shard_map(
        body,
        mesh=mesh,
        in_specs=placed,
        out_specs=(P("layer", None, "plane", None), P("layer", None, "plane", None)),
        check_vma=False,
    )
```

profile of v0, /device:TPU:1, one launch (start us, length us, event | category | flops | bytes accessed | tf_op | source)
XLA Modules:
  0.0 65.4 jit_solution(7252621879696965200)
XLA Ops:
  0.6 0.0 copy-start.8
  1.3 0.0 copy-done.8
  1.3 0.0 copy-start
  1.3 1.2 %copy-done = bf16[512,1024]{1,0:T(8,128)(2,1)S(1)} copy-done((bf16[512,1024]{1,0:T(8,128)(2,1)S(1)}, bf16[512,1024]{1,0:T(8,128)(2,1)}, u32[]{:S(2)}) %copy-start) | copy-done | bytes 1048600
  2.5 0.0 copy-start.1
  2.5 1.2 %copy-done.1 = bf16[512,1024]{1,0:T(8,128)(2,1)S(1)} copy-done((bf16[512,1024]{1,0:T(8,128)(2,1)S(1)}, bf16[512,1024]{1,0:T(8,128)(2,1)}, u32[]{:S(2)}) %copy-start.1) | copy-done | bytes 1048600
  3.8 0.0 copy-start.2
  3.8 1.2 %copy-done.2 = bf16[512,1024]{1,0:T(8,128)(2,1)S(1)} copy-done((bf16[512,1024]{1,0:T(8,128)(2,1)S(1)}, bf16[512,1024]{1,0:T(8,128)(2,1)}, u32[]{:S(2)}) %copy-start.2) | copy-done | bytes 1048600
  5.0 0.0 copy-start.3
  5.0 1.2 %copy-done.3 = bf16[512,1024]{1,0:T(8,128)(2,1)S(1)} copy-done((bf16[512,1024]{1,0:T(8,128)(2,1)S(1)}, bf16[512,1024]{1,0:T(8,128)(2,1)}, u32[]{:S(2)}) %copy-start.3) | copy-done | bytes 1048600
  6.2 0.0 copy-start.4
  6.2 0.8 %copy-done.4 = f32[1,16,512]{2,1,0:T(8,128)S(1)} copy-done((f32[1,16,512]{2,1,0:T(8,128)S(1)}, f32[1,16,512]{2,1,0:T(8,128)}, u32[]{:S(2)}) %copy-start.4) | copy-done | bytes 32792
  7.0 0.0 copy-start.5
  7.0 0.8 %copy-done.5 = f32[1,16,512]{2,1,0:T(8,128)S(1)} copy-done((f32[1,16,512]{2,1,0:T(8,128)S(1)}, f32[1,16,512]{2,1,0:T(8,128)}, u32[]{:S(2)}) %copy-start.5) | copy-done | bytes 32792
  7.7 0.0 copy-start.6
  7.7 0.8 %copy-done.6 = f32[1,16,512]{2,1,0:T(8,128)S(1)} copy-done((f32[1,16,512]{2,1,0:T(8,128)S(1)}, f32[1,16,512]{2,1,0:T(8,128)}, u32[]{:S(2)}) %copy-start.6) | copy-done | bytes 32792
  8.5 0.0 copy-start.7
  8.5 0.8 %copy-done.7 = f32[1,16,512]{2,1,0:T(8,128)S(1)} copy-done((f32[1,16,512]{2,1,0:T(8,128)S(1)}, f32[1,16,512]{2,1,0:T(8,128)}, u32[]{:S(2)}) %copy-start.7) | copy-done | bytes 32792
  9.2 54.9 %fields.1 = (f32[1,3,16,512]{3,2,1,0:T(8,128)S(1)}, f32[1,3,16,512]{3,2,1,0:T(8,128)S(1)}) custom-call(f32[1,16,512]{2,1,0:T(8,128)S(1)} %copy-done.4, f32[1,16,512]{2,1,0:T(8,128)S(1)} %copy-done.5, f32[1,16,512]{2,1,0:T(8,128)S(1)} %copy-done.6, f32[1,16,512]{2,1,0:T(8,128)S(1)} %copy-done.7, f32[1]{0:T(128)S(6)} %copy.14.stiffness, f32[15]{0:T(128)S(1)} %copy-done.8, ...), custom_call_target="tpu_custom_call" | custom-call | flops 1000000000 | bytes 5000000 | tf_op jit(solution)/shard_map/fields/pallas_call | solution.py:442
  64.1 0.6 copy.15
  64.8 0.6 copy.16
Async XLA Ops:
  0.6 0.7 %copy-start.8 = (f32[15]{0:T(128)S(1)}, f32[15]{0:T(128)}, u32[]{:S(2)}) copy-start(f32[15]{0:T(128)} %coupling.1) | copy-start | bytes 184
  1.3 1.2 %copy-start = (bf16[512,1024]{1,0:T(8,128)(2,1)S(1)}, bf16[512,1024]{1,0:T(8,128)(2,1)}, u32[]{:S(2)}) copy-start(bf16[512,1024]{1,0:T(8,128)(2,1)} %constant.11.clone.wxl_any) | copy-start | bytes 3145732
  2.5 1.2 %copy-start.1 = (bf16[512,1024]{1,0:T(8,128)(2,1)S(1)}, bf16[512,1024]{1,0:T(8,128)(2,1)}, u32[]{:S(2)}) copy-start(bf16[512,1024]{1,0:T(8,128)(2,1)} %constant.10.clone.wxh_any) | copy-start | bytes 3145732
  3.8 1.2 %copy-start.2 = (bf16[512,1024]{1,0:T(8,128)(2,1)S(1)}, bf16[512,1024]{1,0:T(8,128)(2,1)}, u32[]{:S(2)}) copy-start(bf16[512,1024]{1,0:T(8,128)(2,1)} %constant.9.clone.wyl_any) | copy-start | bytes 3145732
  5.0 1.2 %copy-start.3 = (bf16[512,1024]{1,0:T(8,128)(2,1)S(1)}, bf16[512,1024]{1,0:T(8,128)(2,1)}, u32[]{:S(2)}) copy-start(bf16[512,1024]{1,0:T(8,128)(2,1)} %constant.8.clone.wyh_any) | copy-start | bytes 3145732
  6.2 0.8 %copy-start.4 = (f32[1,16,512]{2,1,0:T(8,128)S(1)}, f32[1,16,512]{2,1,0:T(8,128)}, u32[]{:S(2)}) copy-start(f32[1,16,512]{2,1,0:T(8,128)} %polar.1) | copy-start | bytes 98308
  7.0 0.8 %copy-start.5 = (f32[1,16,512]{2,1,0:T(8,128)S(1)}, f32[1,16,512]{2,1,0:T(8,128)}, u32[]{:S(2)}) copy-start(f32[1,16,512]{2,1,0:T(8,128)} %azimuth.1) | copy-start | bytes 98308
  7.7 0.8 %copy-start.6 = (f32[1,16,512]{2,1,0:T(8,128)S(1)}, f32[1,16,512]{2,1,0:T(8,128)}, u32[]{:S(2)}) copy-start(f32[1,16,512]{2,1,0:T(8,128)} %saturation.1) | copy-start | bytes 98308
  8.5 0.8 %copy-start.7 = (f32[1,16,512]{2,1,0:T(8,128)S(1)}, f32[1,16,512]{2,1,0:T(8,128)}, u32[]{:S(2)}) copy-start(f32[1,16,512]{2,1,0:T(8,128)} %anisotropy.1) | copy-start | bytes 98308
where the time goes:
time: 66 us; the launch traced here: 65.4 us
  Pallas kernels  54.9 us (83%)
  local copies, waits for them, and re-layouts  9.21 us (14%)
  between operations  1.33 us (2%)
    pallas_call x1, Pallas kernels, body(): pl.pallas_call(kernel, out_shape=(out, out), in_specs=[vmem] * 4 + [smem]...  54.9 us
    unnamed x20, local copies, waits for them, and re-layouts  9.21 us

commit v1 on v0

--- a/solution.py
+++ b/solution.py
@@ -275,8 +275,10 @@
 
 
 def kernel(
-    polar, azimuth, saturation, anisotropy, stiffness, coupling, wyh_any, wyl_any, wxh_any, wxl_any,
+    polar_any, azimuth_any, saturation_any, anisotropy_any, stiffness_any, coupling_any,
+    wyh_any, wyl_any, wxh_any, wxl_any,
     field_out, moment_out,
+    polar, azimuth, saturation, anisotropy, stiffness, coupling,
     wyh, wyl, wxh, wxl, s1, r1, s2, r2, s3, r3, s4, r4, zs, ws, tb, near, edge_out, edge_in, rest,
     load_sem, send_sem, recv_sem, near_send, near_recv, edge_send, edge_recv,
 ):
@@ -288,7 +290,11 @@
 
     loads = [
         pltpu.make_async_copy(src, dst, load_sem.at[i])
-        for i, (src, dst) in enumerate([(wyh_any, wyh), (wyl_any, wyl), (wxh_any, wxh), (wxl_any, wxl)])
+        for i, (src, dst) in enumerate([
+            (polar_any, polar), (azimuth_any, azimuth), (saturation_any, saturation), (wyh_any, wyh), (wyl_any, wyl),
+            (anisotropy_any, anisotropy), (stiffness_any, stiffness), (coupling_any, coupling),
+            (wxh_any, wxh), (wxl_any, wxl),
+        ])
     ]
     for load in loads:
         load.start()
@@ -321,6 +327,8 @@
     for there in (next_plane, last_plane):
         pl.semaphore_signal(barrier, inc=1, device_id=there, device_id_type=MESH)
 
+    loads[0].wait()
+    loads[1].wait()
     m = unit_moment(polar[0], azimuth[0])
     edge_out[...] = jnp.zeros((2, 16, 128), f32)
     for side, row in enumerate((0, 15)):
@@ -329,8 +337,8 @@
                 edge_out[side, c * 4 + lb : c * 4 + lb + 1, :] = m[c][row : row + 1, 128 * lb : 128 * lb + 128]
     s2[...] = jnp.zeros((512, 128), f32)
     s3[...] = jnp.zeros((512, 128), f32)
-    loads[0].wait()
-    loads[1].wait()
+    for load in loads[2:5]:
+        load.wait()
     forward_y(m, saturation[0], wyh, wyl, s1)
 
     pl.semaphore_wait(barrier, RING - 1 + SLAB - 1 + 2)
@@ -377,6 +385,8 @@
     for copy in sides:
         copy.start()
 
+    for load in loads[5:]:
+        load.wait()
     spectral_tables(z * SLAB + f, tb)
     for copy in sides:
         copy.wait_recv()
@@ -404,8 +414,6 @@
     received(r1, 0)
     turn_in(r1, s2)
     slab_send(s2, r2, 1)
-    loads[2].wait()
-    loads[3].wait()
     received(r2, 1)
     transform_x(r2, wxh, wxl, zs)
     couple(zs, tb, ws)
@@ -433,18 +441,20 @@
 
 def body(polar, azimuth, saturation, anisotropy, stiffness, coupling):
     vmem = pl.BlockSpec(memory_space=pltpu.VMEM)
-    smem = pl.BlockSpec(memory_space=pltpu.SMEM)
-    hbm = pl.BlockSpec(memory_space=pl.ANY)
+    hbm = pl.BlockSpec(memory_space=pltpu.HBM)
     out = jax.ShapeDtypeStruct((1, 3, 16, CELLS), f32)
     dma = pltpu.SemaphoreType.DMA
     ring = pltpu.VMEM((RING, 3, 8, 128), f32)
     slab = pltpu.VMEM((SLAB * 16, 128), f32)
+    row_block = pltpu.VMEM((1, 16, CELLS), f32)
     return pl.pallas_call(
         kernel,
         out_shape=(out, out),
-        in_specs=[vmem] * 4 + [smem] * 2 + [hbm] * 4,
+        in_specs=[hbm] * 10,
         out_specs=(vmem, vmem),
         scratch_shapes=[
+            row_block, row_block, row_block, row_block,
+            pltpu.SMEM((1,), f32), pltpu.SMEM((LAYERS - 1,), f32),
             pltpu.VMEM((CELLS, PAD), bf16),
             pltpu.VMEM((CELLS, PAD), bf16),
             pltpu.VMEM((CELLS, PAD), bf16),
@@ -457,10 +467,10 @@
             pltpu.VMEM((2, 16, 128), f32),
             pltpu.VMEM((2, 16, 128), f32),
             pltpu.VMEM((6, 16, CELLS), f32),
-            dma((4,)), dma((4,)), dma((4,)), dma((4,)), dma((4,)), dma((2,)), dma((2,)),
+            dma((10,)), dma((4,)), dma((4,)), dma((4,)), dma((4,)), dma((2,)), dma((2,)),
         ],
         compiler_params=pltpu.CompilerParams(
-            collective_id=0, has_side_effects=True, vmem_limit_bytes=40 * 1024 * 1024
+            collective_id=0, has_side_effects=True, vmem_limit_bytes=60 * 1024 * 1024
         ),
         cost_estimate=pl.CostEstimate(flops=10**9, bytes_accessed=5 * 10**6, transcendentals=0),
         name="fields",

time: 66 us -> 58.5 us (0.89)
  local copies, waits for them, and re-layouts: 9.21 us -> 2.22 us
    unnamed x20 -> x4, local copies, waits for them, and re-layouts: 9.21 us -> 2.22 us
where the time goes in v1:
time: 58.5 us; the launch traced here: 58.3 us
  Pallas kernels  54.8 us (94%)
  local copies, waits for them, and re-layouts  2.22 us (4%)
  between operations  1.29 us (2%)
    pallas_call x1, Pallas kernels, body(): pl.pallas_call(kernel, out_shape=(out, out), in_specs=[hbm] * 10, out_spe...  54.8 us
    unnamed x4, local copies, waits for them, and re-layouts  2.22 us

profile of v1, /device:TPU:1, one launch (start us, length us, event | category | flops | bytes accessed | tf_op | source)
XLA Modules:
  0.0 58.3 jit_solution(15550618632143003616)
XLA Ops:
  1.3 54.8 %fields.1 = (f32[1,3,16,512]{3,2,1,0:T(8,128)}, f32[1,3,16,512]{3,2,1,0:T(8,128)}) custom-call(f32[1,16,512]{2,1,0:T(8,128)} %polar_any.1, f32[1,16,512]{2,1,0:T(8,128)} %azimuth_any.1, f32[1,16,512]{2,1,0:T(8,128)} %saturation_any.1, f32[1,16,512]{2,1,0:T(8,128)} %anisotropy_any.1, f32[1]{0:T(128)S(6)} %copy.14.stiffness_any, f32[15]{0:T(128)} %coupling_any.1, ...), custom_call_target="tpu_custom_call" | custom-call | flops 1000000000 | bytes 5000000 | tf_op jit(solution)/shard_map/fields/pallas_call | solution.py:450
  56.1 0.0 copy-start
  56.1 1.6 %copy.15 = f32[1,3,16,512]{3,2,1,0:T(8,128)} copy(f32[1,3,16,512]{3,2,1,0:T(8,128)} %get-tuple-element.4) | data formatting | bytes 196608
  57.7 0.0 copy-done
  57.7 0.6 %copy.16 = f32[1,3,16,512]{3,2,1,0:T(8,128)} copy(f32[1,3,16,512]{3,2,1,0:T(8,128)S(1)} %copy-done) | data formatting | bytes 196608
Async XLA Ops:
  56.1 1.6 %copy-start = (f32[1,3,16,512]{3,2,1,0:T(8,128)S(1)}, f32[1,3,16,512]{3,2,1,0:T(8,128)}, u32[]{:S(2)}) copy-start(f32[1,3,16,512]{3,2,1,0:T(8,128)} %get-tuple-element.5) | copy-start | bytes 294916

commit v2 on v1

--- a/solution.py
+++ b/solution.py
@@ -21,6 +21,9 @@
 RING = 16
 SLAB = 32
 MESH = pl.DeviceIdType.MESH
+AWAY = [8, 7, 9, 6, 10, 5, 11, 4, 12, 3, 13, 2, 14, 1, 15]
+FAR = [(a, b, dy) for a in range(2) for b in range(2) for dy in range(4)]
+FAR.sort(key=lambda far: -((1 if far[1] else 2 * far[0]) + (0, 1, 2, 1)[far[2]]))
 f32 = jnp.float32
 bf16 = jnp.bfloat16
 
@@ -34,15 +37,15 @@
 @functools.lru_cache(None)
 def transforms():
     column = np.arange(PAD)
-    pair, part = column // 128, column // 64 % 2
-    wave = (2 * pair + column % 2) * SLAB + column // 2 % SLAB
+    pair, core, part = column // 128, column // 64 % 2, column // 32 % 2
+    wave = (2 * pair + column % 2) * SLAB + core * 16 + column // 2 % 16
     place = np.arange(CELLS)
     angle = (place[:, None] * wave[None, :] % PAD) * (2.0 * np.pi / PAD)
     along_y = np.where(part[None, :] == 0, np.cos(angle), np.sin(angle))
     alternating = np.where(place % 2 == 0, 1.0, -1.0)
     along_y[:, (wave == 0) & (part == 1)] = alternating[:, None]
     row = np.arange(CELLS)
-    x = row // 256 * 256 + row // 8 % 16 * 16 + row // 128 % 2 * 8 + row % 8
+    x = row // 256 * 256 + row % 16 * 16 + row // 128 % 2 * 8 + row // 64 % 2 * 4 + row // 16 % 4
     angle = (x[:, None] * np.arange(CELLS)[None, :] % PAD) * (2.0 * np.pi / PAD)
     sine = np.sin(angle)
     sine[:, 0] = np.where(x % 2 == 0, 1.0, -1.0)
@@ -89,23 +92,36 @@
     return lax.broadcasted_iota(jnp.int32, (8, 128), 1) % 2 == 0
 
 
+def low_lanes(rows):
+    return lax.broadcasted_iota(jnp.int32, (rows, 128), 1) < 64
+
+
+def half_turn(x):
+    return pltpu.roll(pltpu.roll(x, 64, 1), 4, 0)
+
+
 def forward_y(m, saturation, wyh, wyl, s1):
     rows = [m[c][8 * h : 8 * h + 8] * saturation[8 * h : 8 * h + 8] for h in range(2) for c in range(3)]
     y = product(jnp.concatenate(rows, 0), wyh, wyl, False)
-    even = even_lanes()
+    even, low = even_lanes(), low_lanes(8)
     for c in range(3):
         for p in range(8):
             upper = y[8 * c : 8 * c + 8, 128 * p : 128 * p + 128]
             lower = y[24 + 8 * c : 32 + 8 * c, 128 * p : 128 * p + 128]
-            s1[2 * p, c] = jnp.where(even, upper, pltpu.roll(lower, 1, 1))
-            s1[2 * p + 1, c] = jnp.where(even, pltpu.roll(upper, 127, 1), lower)
-
-
-def turn_in(r1, s2):
-    for c in range(3):
-        block = r1[:, c].reshape(128, 128).T
+            first = jnp.where(even, upper, pltpu.roll(lower, 1, 1))
+            second = jnp.where(even, pltpu.roll(upper, 127, 1), lower)
+            for z, tile in ((2 * p, first), (2 * p + 1, second)):
+                turned = half_turn(tile)
+                s1[pl.ds(z * 12 + c * 4, 4), :] = jnp.where(low, tile, turned)[:4]
+                s1[pl.ds(192 + z * 12 + c * 4, 4), :] = jnp.where(low, turned, tile)[4:]
+
+
+def turn_in(k, r1, s2):
+    for c in range(3):
+        x = jnp.concatenate([r1[pl.ds(k * 192 + c * 4 + r, 16, stride=12), :] for r in range(4)], 0)
+        block = jnp.concatenate([x, pltpu.roll(x, 64, 1)], 0).T
         for b in range(2):
-            s2[pl.ds(2 * c + b, 64, stride=8), :] = block[64 * b : 64 * b + 64]
+            s2[pl.ds(k * 192 + 2 * c + b, 32, stride=6), :] = block[32 * b : 32 * b + 32]
 
 
 def spectral_tables(fy, tb):
@@ -153,7 +169,7 @@
     columns = []
     for x_lo in range(2):
         for h in range(2):
-            parts = [r2[pl.ds(x_lo * 16 + h * 8 + q, 16, stride=32), :] for q in range(6)]
+            parts = [r2[pl.ds(x_lo * 12 + h * 6 + q, 16, stride=24), :] for q in range(6)]
             columns.append(jnp.concatenate(parts, 0))
     z = product(jnp.concatenate(columns, 1), wxh, wxl, False)
     for c in range(3):
@@ -225,22 +241,32 @@
         for h in range(2):
             lane = (x_lo * 2 + h) * 128
             for q in range(6):
-                s3[pl.ds(x_lo * 16 + h * 8 + q, 16, stride=32), :] = out[16 * q : 16 * q + 16, lane : lane + 128]
-
-
-def turn_out(r3, s4):
-    for c in range(3):
-        parts = [r3[pl.ds(2 * c + b, 64, stride=8), :] for b in range(2)]
-        s4[:, c] = jnp.concatenate(parts, 0).T.reshape(16, 8, 128)
+                s3[pl.ds(x_lo * 12 + h * 6 + q, 16, stride=24), :] = out[16 * q : 16 * q + 16, lane : lane + 128]
+
+
+def turn_out(k, r3, s4):
+    low = low_lanes(64)
+    for c in range(3):
+        parts = [r3[pl.ds(k * 192 + 2 * c + b, 32, stride=6), :] for b in range(2)]
+        block = jnp.concatenate(parts + parts, 0).T
+        block = jnp.where(low, block[:64], block[64:])
+        for r in range(4):
+            s4[pl.ds(k * 192 + c * 4 + r, 16, stride=12), :] = block[16 * r : 16 * r + 16]
 
 
 def inverse_y(r4, wyh, wyl):
     even = even_lanes()
+    kept = low_lanes(8) == (lax.broadcasted_iota(jnp.int32, (8, 128), 0) < 4)
+
+    def tile(z, c):
+        both = jnp.concatenate([r4[pl.ds(k * 192 + z * 12 + c * 4, 4), :] for k in range(2)], 0)
+        return jnp.where(kept, both, half_turn(both))
+
     upper, lower = [], []
     for c in range(3):
         up, low = [], []
         for p in range(8):
-            first, second = r4[2 * p, c], r4[2 * p + 1, c]
+            first, second = tile(2 * p, c), tile(2 * p + 1, c)
             up.append(jnp.where(even, first, pltpu.roll(second, 1, 1)))
             low.append(jnp.where(even, pltpu.roll(first, 127, 1), second))
         upper.append(jnp.concatenate(up, 1))
@@ -286,7 +312,11 @@
     p = lax.axis_index("plane")
     z = lax.rem(p, RING)
     x_lo = lax.div(p, RING)
-    f = t * 2 + x_lo
+    core = lax.rem(t, 2)
+    y = lax.rem(lax.div(t, 2), 4)
+    x_hi = lax.div(t, 8)
+    source = t * 2 + x_lo
+    owner = core * 16 + lax.div(t, 2) * 2 + x_lo
 
     loads = [
         pltpu.make_async_copy(src, dst, load_sem.at[i])
@@ -299,14 +329,16 @@
     for load in loads:
         load.start()
 
-    def ring_device(i):
-        dist = RING // 2 - lax.div(i + 1, 2)
-        there = lax.rem(z + jnp.where(lax.rem(i, 2) == 1, dist, RING - dist), RING)
+    def ring_device(away):
+        there = lax.rem(z + away, RING)
         return there, (t, x_lo * RING + there)
 
-    def slab_device(i):
-        there = lax.rem(f + 1 + i, SLAB)
-        return there, (lax.div(there, 2), lax.rem(there, 2) * RING + z)
+    def slab_device(far, there_core):
+        a, b, dy = far
+        there_x = lax.rem(x_lo + b, 2)
+        pair = lax.rem(x_hi + a, 2) * 4 + lax.rem(y + dy, 4)
+        there_t = pair * 2 + there_core
+        return there_t * 2 + there_x, there_core * 16 + pair * 2 + there_x, (there_t, there_x * RING + z)
 
     next_plane = (t, lax.rem(p + 1, 2 * RING))
     last_plane = (t, lax.rem(p + 2 * RING - 1, 2 * RING))
@@ -315,17 +347,17 @@
 
     barrier = pltpu.get_barrier_semaphore()
 
-    def greet(where):
-        def one(i, carry):
-            pl.semaphore_signal(barrier, inc=1, device_id=where(i)[1], device_id_type=MESH)
-            return carry
-
-        return one
-
-    lax.fori_loop(0, RING - 1, greet(ring_device), 0)
-    lax.fori_loop(0, SLAB - 1, greet(slab_device), 0)
+    def greet(there):
+        pl.semaphore_signal(barrier, inc=1, device_id=there, device_id_type=MESH)
+
+    for away in AWAY:
+        greet(ring_device(away)[1])
+    for far in FAR:
+        greet(slab_device(far, 1 - core)[2])
+        if any(far):
+            greet(slab_device(far, core)[2])
     for there in (next_plane, last_plane):
-        pl.semaphore_signal(barrier, inc=1, device_id=there, device_id_type=MESH)
+        greet(there)
 
     loads[0].wait()
     loads[1].wait()
@@ -335,8 +367,6 @@
         for c in range(3):
             for lb in range(4):
                 edge_out[side, c * 4 + lb : c * 4 + lb + 1, :] = m[c][row : row + 1, 128 * lb : 128 * lb + 128]
-    s2[...] = jnp.zeros((512, 128), f32)
-    s3[...] = jnp.zeros((512, 128), f32)
     for load in loads[2:5]:
         load.wait()
     forward_y(m, saturation[0], wyh, wyl, s1)
@@ -348,31 +378,47 @@
             src_ref=src, dst_ref=dst, send_sem=sem[0], recv_sem=sem[1], device_id=there, device_id_type=MESH
         )
 
-    def ring_send(src, dst, n):
-        def one(i, carry):
-            there, device = ring_device(i)
-            remote(src.at[there], dst.at[z], (send_sem.at[n], recv_sem.at[n]), device).start()
-            return carry
-
-        lax.fori_loop(0, RING - 1, one, 0)
-        pltpu.make_async_copy(src.at[z], dst.at[z], recv_sem.at[n]).start()
-
     def rows_of(ref, i):
-        return ref.at[pl.ds(pl.multiple_of(i * 16, 16), 16)]
-
-    def slab_send(src, dst, n):
-        def one(i, carry):
-            there, device = slab_device(i)
-            remote(rows_of(src, there), rows_of(dst, f), (send_sem.at[n], recv_sem.at[n]), device).start()
-            return carry
-
-        lax.fori_loop(0, SLAB - 1, one, 0)
-        pltpu.make_async_copy(rows_of(src, f), rows_of(dst, f), recv_sem.at[n]).start()
-
-    def received(dst, n):
-        pltpu.make_async_copy(dst, dst, recv_sem.at[n]).wait()
-
-    ring_send(s1, r1, 0)
+        return ref.at[pl.ds(pl.multiple_of(i * 12, 4), 12)]
+
+    def ring_send(src, dst, n, k, arrival):
+        for away in AWAY:
+            there, device = ring_device(away)
+            sems = (send_sem.at[n], recv_sem.at[arrival])
+            remote(rows_of(src, k * 16 + there), rows_of(dst, k * 16 + z), sems, device).start()
+        pltpu.make_async_copy(rows_of(src, k * 16 + z), rows_of(dst, k * 16 + z), recv_sem.at[arrival]).start()
+
+    def slab_send(k):
+        sems = (send_sem.at[1], recv_sem.at[2])
+        for far in FAR:
+            _, there, device = slab_device(far, k)
+            if any(far):
+                remote(rows_of(s2, there), rows_of(r2, source), sems, device).start()
+            else:
+
+                @pl.when(core == k)
+                def _():
+                    pltpu.make_async_copy(rows_of(s2, owner), rows_of(r2, source), recv_sem.at[2]).start()
+
+                @pl.when(core != k)
+                def _():
+                    remote(rows_of(s2, there), rows_of(r2, source), sems, device).start()
+
+    def slab_return():
+        sems = (send_sem.at[2], recv_sem.at[3 + core])
+        for far in FAR:
+            for there_core in (core, 1 - core):
+                there, _, device = slab_device(far, there_core)
+                if any(far) or there_core is not core:
+                    remote(rows_of(s3, there), rows_of(r3, owner), sems, device).start()
+        pltpu.make_async_copy(rows_of(s3, source), rows_of(r3, owner), recv_sem.at[3 + core]).start()
+
+    def received(dst, n, rows=192):
+        part = dst.at[pl.ds(0, rows)]
+        pltpu.make_async_copy(part, part, recv_sem.at[n]).wait()
+
+    for k in range(2):
+        ring_send(s1, r1, 0, k, k)
     sides = []
     for i, (ref, side, there) in enumerate(
         [(polar, 0, next_layer), (azimuth, 0, next_layer), (polar, 1, last_layer), (azimuth, 1, last_layer)]
@@ -387,7 +433,11 @@
 
     for load in loads[5:]:
         load.wait()
-    spectral_tables(z * SLAB + f, tb)
+    spectral_tables(z * SLAB + owner, tb)
+    for k in range(2):
+        received(r1, k)
+        turn_in(k, r1, s2)
+        slab_send(k)
     for copy in sides:
         copy.wait_recv()
     lower_m = unit_moment(near[0, 0], near[0, 1])
@@ -411,18 +461,17 @@
         rest[c] = fields[c]
         rest[3 + c] = m[c]
 
-    received(r1, 0)
-    turn_in(r1, s2)
-    slab_send(s2, r2, 1)
-    received(r2, 1)
+    received(r2, 2, 384)
     transform_x(r2, wxh, wxl, zs)
     couple(zs, tb, ws)
     return_x(zs, wxh, wxl, s3)
-    slab_send(s3, r3, 2)
-    received(r3, 2)
-    turn_out(r3, s4)
-    ring_send(s4, r4, 3)
-    received(r4, 3)
+    slab_return()
+    for k in range(2):
+        received(r3, 3 + k)
+        turn_out(k, r3, s4)
+        ring_send(s4, r4, 3, k, 5 + k)
+    received(r4, 5)
+    received(r4, 6)
     demag = inverse_y(r4, wyh, wyl)
     m = [rest[3 + c] for c in range(3)]
     field = [demag[c] + rest[c] for c in range(3)]
@@ -433,9 +482,8 @@
 
     for copy in sides:
         copy.wait_send()
-    ring_part = s1.at[pl.ds(0, RING - 1)]
-    slab_part = s2.at[pl.ds(0, 16 * (SLAB - 1))]
-    for n, part in ((0, ring_part), (1, slab_part), (2, slab_part), (3, ring_part)):
+    for n, rows in ((0, 360), (1, 372), (2, 372), (3, 360)):
+        part = s1.at[pl.ds(0, rows)]
         pltpu.make_async_copy(part, part, send_sem.at[n]).wait()
 
 
@@ -444,8 +492,7 @@
     hbm = pl.BlockSpec(memory_space=pltpu.HBM)
     out = jax.ShapeDtypeStruct((1, 3, 16, CELLS), f32)
     dma = pltpu.SemaphoreType.DMA
-    ring = pltpu.VMEM((RING, 3, 8, 128), f32)
-    slab = pltpu.VMEM((SLAB * 16, 128), f32)
+    block = pltpu.VMEM((SLAB * 12, 128), f32)
     row_block = pltpu.VMEM((1, 16, CELLS), f32)
     return pl.pallas_call(
         kernel,
@@ -459,7 +506,7 @@
             pltpu.VMEM((CELLS, PAD), bf16),
             pltpu.VMEM((CELLS, PAD), bf16),
             pltpu.VMEM((CELLS, PAD), bf16),
-            ring, ring, slab, slab, slab, slab, ring, ring,
+            block, block, block, block, block, block, block, block,
             pltpu.VMEM((3 * 2 * 16 * 8, 128), f32),
             pltpu.VMEM((2, LAYERS, 4, 8, 128), f32),
             pltpu.VMEM((2, 8, 8, 128), f32),
@@ -467,7 +514,7 @@
             pltpu.VMEM((2, 16, 128), f32),
             pltpu.VMEM((2, 16, 128), f32),
             pltpu.VMEM((6, 16, CELLS), f32),
-            dma((10,)), dma((4,)), dma((4,)), dma((4,)), dma((4,)), dma((2,)), dma((2,)),
+            dma((10,)), dma((4,)), dma((7,)), dma((4,)), dma((4,)), dma((2,)), dma((2,)),
         ],
         compiler_params=pltpu.CompilerParams(
             collective_id=0, has_side_effects=True, vmem_limit_bytes=60 * 1024 * 1024

time: 58.5 us -> 53.6 us (0.916); the launches traced: 58.3 us -> 52.6 us
  Pallas kernels: 54.8 us -> 49.1 us
    pallas_call x1, Pallas kernels: 54.8 us -> 49.1 us  [body(): pl.pallas_call(kernel, out_shape=(out, out), in_specs=[hbm] * 10, out_spe...]
where the time goes in v2:
time: 53.6 us; the launch traced here: 52.6 us
  Pallas kernels  49.1 us (92%)
  local copies, waits for them, and re-layouts  2.22 us (4%)
  between operations  1.29 us (2%)
    pallas_call x1, Pallas kernels, body(): pl.pallas_call(kernel, out_shape=(out, out), in_specs=[hbm] * 10, out_spe...  49.1 us
    unnamed x4, local copies, waits for them, and re-layouts  2.22 us

profile of v2, /device:TPU:1, one launch (start us, length us, event | category | flops | bytes accessed | tf_op | source)
XLA Modules:
  0.0 52.6 jit_solution(12805455974411220473)
XLA Ops:
  1.3 49.1 %fields.1 = (f32[1,3,16,512]{3,2,1,0:T(8,128)}, f32[1,3,16,512]{3,2,1,0:T(8,128)}) custom-call(f32[1,16,512]{2,1,0:T(8,128)} %polar_any.1, f32[1,16,512]{2,1,0:T(8,128)} %azimuth_any.1, f32[1,16,512]{2,1,0:T(8,128)} %saturation_any.1, f32[1,16,512]{2,1,0:T(8,128)} %anisotropy_any.1, f32[1]{0:T(128)S(6)} %copy.14.stiffness_any, f32[15]{0:T(128)} %coupling_any.1, ...), custom_call_target="tpu_custom_call" | custom-call | flops 1000000000 | bytes 5000000 | tf_op jit(solution)/shard_map/fields/pallas_call | solution.py:497
  50.4 0.0 copy-start
  50.4 1.6 %copy.15 = f32[1,3,16,512]{3,2,1,0:T(8,128)} copy(f32[1,3,16,512]{3,2,1,0:T(8,128)} %get-tuple-element.4) | data formatting | bytes 196608
  51.9 0.0 copy-done
  51.9 0.6 %copy.16 = f32[1,3,16,512]{3,2,1,0:T(8,128)} copy(f32[1,3,16,512]{3,2,1,0:T(8,128)S(1)} %copy-done) | data formatting | bytes 196608
Async XLA Ops:
  50.4 1.6 %copy-start = (f32[1,3,16,512]{3,2,1,0:T(8,128)S(1)}, f32[1,3,16,512]{3,2,1,0:T(8,128)}, u32[]{:S(2)}) copy-start(f32[1,3,16,512]{3,2,1,0:T(8,128)} %get-tuple-element.5) | copy-start | bytes 294916

commit v3 on v2

--- a/solution.py
+++ b/solution.py
@@ -37,8 +37,8 @@
 @functools.lru_cache(None)
 def transforms():
     column = np.arange(PAD)
-    pair, core, part = column // 128, column // 64 % 2, column // 32 % 2
-    wave = (2 * pair + column % 2) * SLAB + core * 16 + column // 2 % 16
+    core, part = column // 512, column // 32 % 2
+    wave = (column // 64 % 8 * 2 + column % 2) * SLAB + core * 16 + column // 2 % 16
     place = np.arange(CELLS)
     angle = (place[:, None] * wave[None, :] % PAD) * (2.0 * np.pi / PAD)
     along_y = np.where(part[None, :] == 0, np.cos(angle), np.sin(angle))
@@ -76,15 +76,15 @@
     return sin_p * (1.0 - 2.0 * s * s), sin_p * (2.0 * s * c), cos_p
 
 
-def product(left, high_ref, low_ref, transposed):
-    high = left.astype(bf16)
-    low = (left - high.astype(f32)).astype(bf16)
+def product(left, high, low, transposed):
+    left_high = left.astype(bf16)
+    left_low = (left - left_high.astype(f32)).astype(bf16)
     rows = left.shape[0]
     dims = (((1,), (1 if transposed else 0,)), ((), ()))
     both = lax.dot_general(
-        jnp.concatenate([high, low], 0), high_ref[...], dims, preferred_element_type=f32
+        jnp.concatenate([left_high, left_low], 0), high, dims, preferred_element_type=f32
     )
-    rest = lax.dot_general(high, low_ref[...], dims, preferred_element_type=f32)
+    rest = lax.dot_general(left_high, low, dims, preferred_element_type=f32)
     return both[:rows] + both[rows:] + rest
 
 
@@ -102,7 +102,7 @@
 
 def forward_y(m, saturation, wyh, wyl, s1):
     rows = [m[c][8 * h : 8 * h + 8] * saturation[8 * h : 8 * h + 8] for h in range(2) for c in range(3)]
-    y = product(jnp.concatenate(rows, 0), wyh, wyl, False)
+    y = product(jnp.concatenate(rows, 0), wyh[...], wyl[...], False)
     even, low = even_lanes(), low_lanes(8)
     for c in range(3):
         for p in range(8):
@@ -110,10 +110,11 @@
             lower = y[24 + 8 * c : 32 + 8 * c, 128 * p : 128 * p + 128]
             first = jnp.where(even, upper, pltpu.roll(lower, 1, 1))
             second = jnp.where(even, pltpu.roll(upper, 127, 1), lower)
-            for z, tile in ((2 * p, first), (2 * p + 1, second)):
+            for z, tile in ((p % 4 * 4, first), (p % 4 * 4 + 1, second)):
                 turned = half_turn(tile)
-                s1[pl.ds(z * 12 + c * 4, 4), :] = jnp.where(low, tile, turned)[:4]
-                s1[pl.ds(192 + z * 12 + c * 4, 4), :] = jnp.where(low, turned, tile)[4:]
+                row = (p // 4 * 16 + z) * 12 + c * 4
+                s1[pl.ds(row, 4), :] = jnp.where(low, tile, turned)[:4]
+                s1[pl.ds(row + 24, 4), :] = jnp.where(low, turned, tile)[4:]
 
 
 def turn_in(k, r1, s2):
@@ -171,7 +172,7 @@
         for h in range(2):
             parts = [r2[pl.ds(x_lo * 12 + h * 6 + q, 16, stride=24), :] for q in range(6)]
             columns.append(jnp.concatenate(parts, 0))
-    z = product(jnp.concatenate(columns, 1), wxh, wxl, False)
+    z = product(jnp.concatenate(columns, 1), wxh[...], wxl[...], False)
     for c in range(3):
         for cls, (a, b) in enumerate(ORDER_X if c == 0 else ORDER):
             for tg in range(2):
@@ -236,7 +237,7 @@
                     zs[pl.ds(tile_row(c, tg, order.index((a, b)), lb), 8), :] for a in range(2) for lb in range(4)
                 ]
                 rows.append(jnp.concatenate(lanes, 1))
-    out = product(jnp.concatenate(rows, 0), wxh, wxl, True)
+    out = product(jnp.concatenate(rows, 0), wxh[...], wxl[...], True)
     for x_lo in range(2):
         for h in range(2):
             lane = (x_lo * 2 + h) * 128
@@ -254,25 +255,26 @@
             s4[pl.ds(k * 192 + c * 4 + r, 16, stride=12), :] = block[16 * r : 16 * r + 16]
 
 
-def inverse_y(r4, wyh, wyl):
+def inverse_y(k, r4, wyh, wyl):
     even = even_lanes()
     kept = low_lanes(8) == (lax.broadcasted_iota(jnp.int32, (8, 128), 0) < 4)
 
     def tile(z, c):
-        both = jnp.concatenate([r4[pl.ds(k * 192 + z * 12 + c * 4, 4), :] for k in range(2)], 0)
+        row = k * 192 + z * 12 + c * 4
+        both = jnp.concatenate([r4[pl.ds(row, 4), :], r4[pl.ds(row + 24, 4), :]], 0)
         return jnp.where(kept, both, half_turn(both))
 
     upper, lower = [], []
     for c in range(3):
         up, low = [], []
-        for p in range(8):
-            first, second = tile(2 * p, c), tile(2 * p + 1, c)
+        for p in range(4):
+            first, second = tile(4 * p, c), tile(4 * p + 1, c)
             up.append(jnp.where(even, first, pltpu.roll(second, 1, 1)))
             low.append(jnp.where(even, pltpu.roll(first, 127, 1), second))
         upper.append(jnp.concatenate(up, 1))
         lower.append(jnp.concatenate(low, 1))
-    out = product(jnp.concatenate(upper + lower, 0), wyh, wyl, True)
-    return [jnp.concatenate([out[8 * c : 8 * c + 8], out[24 + 8 * c : 32 + 8 * c]], 0) for c in range(3)]
+    columns = slice(512 * k, 512 * k + 512)
+    return product(jnp.concatenate(upper + lower, 0), wyh[:, columns], wyl[:, columns], True)
 
 
 def cross_product(a, b):
@@ -471,10 +473,13 @@
         turn_out(k, r3, s4)
         ring_send(s4, r4, 3, k, 5 + k)
     received(r4, 5)
+    demag = inverse_y(0, r4, wyh, wyl)
     received(r4, 6)
-    demag = inverse_y(r4, wyh, wyl)
+    demag = demag + inverse_y(1, r4, wyh, wyl)
     m = [rest[3 + c] for c in range(3)]
-    field = [demag[c] + rest[c] for c in range(3)]
+    field = [
+        jnp.concatenate([demag[8 * c : 8 * c + 8], demag[24 + 8 * c : 32 + 8 * c]], 0) + rest[c] for c in range(3)
+    ]
     moment = step(m, field)
     for c in range(3):
         field_out[0, c] = field[c]
@@ -490,7 +495,7 @@
 def body(polar, azimuth, saturation, anisotropy, stiffness, coupling):
     vmem = pl.BlockSpec(memory_space=pltpu.VMEM)
     hbm = pl.BlockSpec(memory_space=pltpu.HBM)
-    out = jax.ShapeDtypeStruct((1, 3, 16, CELLS), f32)
+    out = pltpu.VMEM((1, 3, 16, CELLS), f32)
     dma = pltpu.SemaphoreType.DMA
     block = pltpu.VMEM((SLAB * 12, 128), f32)
     row_block = pltpu.VMEM((1, 16, CELLS), f32)

time: 53.6 us -> 51.6 us (0.963)
  Pallas kernels: 49.1 us -> 48.1 us
  local copies, waits for them, and re-layouts: 2.22 us -> 1.28 us
    pallas_call x1, Pallas kernels: 49.1 us -> 48.1 us  [body(): pl.pallas_call(kernel, out_shape=(out, out), in_specs=[hbm] * 10, out_spe...]
    unnamed x4 -> x2, local copies, waits for them, and re-layouts: 2.22 us -> 1.28 us
where the time goes in v3:
time: 51.6 us; the launch traced here: 50.6 us
  Pallas kernels  48.1 us (93%)
  between operations  1.29 us (2%)
  local copies, waits for them, and re-layouts  1.28 us (2%)
    pallas_call x1, Pallas kernels, body(): pl.pallas_call(kernel, out_shape=(out, out), in_specs=[hbm] * 10, out_spe...  48.1 us
    unnamed x2, local copies, waits for them, and re-layouts  1.28 us

profile of v3, /device:TPU:1, one launch (start us, length us, event | category | flops | bytes accessed | tf_op | source)
XLA Modules:
  0.0 50.6 jit_solution(15651612396638779022)
XLA Ops:
  1.3 48.1 %fields.1 = (f32[1,3,16,512]{3,2,1,0:T(8,128)S(1)}, f32[1,3,16,512]{3,2,1,0:T(8,128)S(1)}) custom-call(f32[1,16,512]{2,1,0:T(8,128)} %polar_any.1, f32[1,16,512]{2,1,0:T(8,128)} %azimuth_any.1, f32[1,16,512]{2,1,0:T(8,128)} %saturation_any.1, f32[1,16,512]{2,1,0:T(8,128)} %anisotropy_any.1, f32[1]{0:T(128)S(6)} %copy.16.stiffness_any, f32[15]{0:T(128)} %coupling_any.1, ...), custom_call_target="tpu_custom_call" | custom-call | flops 1000000000 | bytes 5000000 | tf_op jit(solution)/shard_map/fields/pallas_call | solution.py:502
  49.3 0.6 %copy.14 = f32[1,3,16,512]{3,2,1,0:T(8,128)} copy(f32[1,3,16,512]{3,2,1,0:T(8,128)S(1)} %get-tuple-element.2) | data formatting | bytes 196608
  50.0 0.6 %copy.15 = f32[1,3,16,512]{3,2,1,0:T(8,128)} copy(f32[1,3,16,512]{3,2,1,0:T(8,128)S(1)} %get-tuple-element.3) | data formatting | bytes 196608

commit v4 on v3

--- a/solution.py
+++ b/solution.py
@@ -21,6 +21,7 @@
 RING = 16
 SLAB = 32
 MESH = pl.DeviceIdType.MESH
+NEAR = [4, 12, 3, 13, 2, 14, 1, 15]
 AWAY = [8, 7, 9, 6, 10, 5, 11, 4, 12, 3, 13, 2, 14, 1, 15]
 FAR = [(a, b, dy) for a in range(2) for b in range(2) for dy in range(4)]
 FAR.sort(key=lambda far: -((1 if far[1] else 2 * far[0]) + (0, 1, 2, 1)[far[2]]))
@@ -112,9 +113,12 @@
             second = jnp.where(even, pltpu.roll(upper, 127, 1), lower)
             for z, tile in ((p % 4 * 4, first), (p % 4 * 4 + 1, second)):
                 turned = half_turn(tile)
-                row = (p // 4 * 16 + z) * 12 + c * 4
-                s1[pl.ds(row, 4), :] = jnp.where(low, tile, turned)[:4]
-                s1[pl.ds(row + 24, 4), :] = jnp.where(low, turned, tile)[4:]
+                row = (p // 4 * 20 + z) * 12 + c * 4
+                blocks = (jnp.where(low, tile, turned)[:4], jnp.where(low, turned, tile)[4:])
+                for place, part in zip((row, row + 24), blocks):
+                    s1[pl.ds(place, 4), :] = part
+                    if p % 4 == 0:
+                        s1[pl.ds(place + 192, 4), :] = part
 
 
 def turn_in(k, r1, s2):
@@ -307,8 +311,8 @@
     wyh_any, wyl_any, wxh_any, wxl_any,
     field_out, moment_out,
     polar, azimuth, saturation, anisotropy, stiffness, coupling,
-    wyh, wyl, wxh, wxl, s1, r1, s2, r2, s3, r3, s4, r4, zs, ws, tb, near, edge_out, edge_in, rest,
-    load_sem, send_sem, recv_sem, near_send, near_recv, edge_send, edge_recv,
+    wyh, wyl, wxh, wxl, s1, r1, s2, r2, s3, r3, s4, r4, zs, ws, tb, near, edge_out, edge_in, rest, relay,
+    load_sem, send_sem, recv_sem, near_send, near_recv, edge_send, edge_recv, relay_sem,
 ):
     t = lax.axis_index("layer")
     p = lax.axis_index("plane")
@@ -320,6 +324,36 @@
     source = t * 2 + x_lo
     owner = core * 16 + lax.div(t, 2) * 2 + x_lo
 
+    def ring_device(away):
+        there = lax.rem(z + away, RING)
+        return there, (t, x_lo * RING + there)
+
+    def slab_device(far, there_core):
+        a, b, dy = far
+        there_x = lax.rem(x_lo + b, 2)
+        pair = lax.rem(x_hi + a, 2) * 4 + lax.rem(y + dy, 4)
+        there_t = pair * 2 + there_core
+        return there_t * 2 + there_x, there_core * 16 + pair * 2 + there_x, (there_t, there_x * RING + z)
+
+    next_plane = (t, lax.rem(p + 1, 2 * RING))
+    last_plane = (t, lax.rem(p + 2 * RING - 1, 2 * RING))
+    next_layer = (lax.rem(t + 1, LAYERS), p)
+    last_layer = (lax.rem(t + LAYERS - 1, LAYERS), p)
+
+    barrier = pltpu.get_barrier_semaphore()
+
+    def greet(there):
+        pl.semaphore_signal(barrier, inc=1, device_id=there, device_id_type=MESH)
+
+    for away in NEAR:
+        greet(ring_device(away)[1])
+    for far in FAR:
+        greet(slab_device(far, 1 - core)[2])
+        if any(far):
+            greet(slab_device(far, core)[2])
+    for there in (next_plane, last_plane):
+        greet(there)
+
     loads = [
         pltpu.make_async_copy(src, dst, load_sem.at[i])
         for i, (src, dst) in enumerate([
@@ -330,36 +364,6 @@
     ]
     for load in loads:
         load.start()
-
-    def ring_device(away):
-        there = lax.rem(z + away, RING)
-        return there, (t, x_lo * RING + there)
-
-    def slab_device(far, there_core):
-        a, b, dy = far
-        there_x = lax.rem(x_lo + b, 2)
-        pair = lax.rem(x_hi + a, 2) * 4 + lax.rem(y + dy, 4)
-        there_t = pair * 2 + there_core
-        return there_t * 2 + there_x, there_core * 16 + pair * 2 + there_x, (there_t, there_x * RING + z)
-
-    next_plane = (t, lax.rem(p + 1, 2 * RING))
-    last_plane = (t, lax.rem(p + 2 * RING - 1, 2 * RING))
-    next_layer = (lax.rem(t + 1, LAYERS), p)
-    last_layer = (lax.rem(t + LAYERS - 1, LAYERS), p)
-
-    barrier = pltpu.get_barrier_semaphore()
-
-    def greet(there):
-        pl.semaphore_signal(barrier, inc=1, device_id=there, device_id_type=MESH)
-
-    for away in AWAY:
-        greet(ring_device(away)[1])
-    for far in FAR:
-        greet(slab_device(far, 1 - core)[2])
-        if any(far):
-            greet(slab_device(far, core)[2])
-    for there in (next_plane, last_plane):
-        greet(there)
 
     loads[0].wait()
     loads[1].wait()
@@ -373,7 +377,7 @@
         load.wait()
     forward_y(m, saturation[0], wyh, wyl, s1)
 
-    pl.semaphore_wait(barrier, RING - 1 + SLAB - 1 + 2)
+    pl.semaphore_wait(barrier, len(NEAR) + SLAB - 1 + 2)
 
     def remote(src, dst, sem, there):
         return pltpu.make_async_remote_copy(
@@ -419,8 +423,41 @@
         part = dst.at[pl.ds(0, rows)]
         pltpu.make_async_copy(part, part, recv_sem.at[n]).wait()
 
+    before, from_before = ring_device(12)
+    after, from_after = ring_device(4)
+
+    def span(ref, first, count):
+        return ref.at[pl.ds(pl.multiple_of(first * 12, 4), count * 12)]
+
+    def send_far(k):
+        up = span(s1, k * 20 + ring_device(5)[0], 4)
+        down = span(s1, k * 20 + ring_device(9)[0], 3)
+        remote(up, span(relay, k * 7, 4), (send_sem.at[0], relay_sem.at[2 * k]), from_after).start()
+        remote(down, span(relay, k * 7 + 4, 3), (send_sem.at[0], relay_sem.at[2 * k + 1]), from_before).start()
+
+    def send_near(k):
+        for away in NEAR:
+            there, device = ring_device(away)
+            sems = (send_sem.at[0], recv_sem.at[k])
+            remote(span(s1, k * 20 + there, 1), rows_of(r1, k * 16 + z), sems, device).start()
+        pltpu.make_async_copy(span(s1, k * 20 + z, 1), rows_of(r1, k * 16 + z), recv_sem.at[k]).start()
+
+    def pass_on(k):
+        sems = (send_sem.at[4], recv_sem.at[k])
+        for side, first, count, source_z, aways in (
+            (0, k * 7, 4, before, (1, 2, 3, 4)), (1, k * 7 + 4, 3, after, (13, 14, 15)),
+        ):
+            arrived = span(relay, first, count)
+            pltpu.make_async_copy(arrived, arrived, relay_sem.at[2 * k + side]).wait()
+            order = sorted(range(count), key=lambda i: -min(aways[i], RING - aways[i]))
+            for i in order:
+                _, device = ring_device(aways[i])
+                remote(span(relay, first + i, 1), rows_of(r1, k * 16 + source_z), sems, device).start()
+
     for k in range(2):
-        ring_send(s1, r1, 0, k, k)
+        send_far(k)
+    for k in range(2):
+        send_near(k)
     sides = []
     for i, (ref, side, there) in enumerate(
         [(polar, 0, next_layer), (azimuth, 0, next_layer), (polar, 1, last_layer), (azimuth, 1, last_layer)]
@@ -436,6 +473,8 @@
     for load in loads[5:]:
         load.wait()
     spectral_tables(z * SLAB + owner, tb)
+    for k in range(2):
+        pass_on(k)
     for k in range(2):
         received(r1, k)
         turn_in(k, r1, s2)
@@ -487,7 +526,7 @@
 
     for copy in sides:
         copy.wait_send()
-    for n, rows in ((0, 360), (1, 372), (2, 372), (3, 360)):
+    for n, rows in ((0, 360), (1, 372), (2, 372), (3, 360), (4, 168)):
         part = s1.at[pl.ds(0, rows)]
         pltpu.make_async_copy(part, part, send_sem.at[n]).wait()
 
@@ -511,7 +550,7 @@
             pltpu.VMEM((CELLS, PAD), bf16),
             pltpu.VMEM((CELLS, PAD), bf16),
             pltpu.VMEM((CELLS, PAD), bf16),
-            block, block, block, block, block, block, block, block,
+            pltpu.VMEM((2 * 20 * 12, 128), f32), block, block, block, block, block, block, block,
             pltpu.VMEM((3 * 2 * 16 * 8, 128), f32),
             pltpu.VMEM((2, LAYERS, 4, 8, 128), f32),
             pltpu.VMEM((2, 8, 8, 128), f32),
@@ -519,7 +558,8 @@
             pltpu.VMEM((2, 16, 128), f32),
             pltpu.VMEM((2, 16, 128), f32),
             pltpu.VMEM((6, 16, CELLS), f32),
-            dma((10,)), dma((4,)), dma((7,)), dma((4,)), dma((4,)), dma((2,)), dma((2,)),
+            pltpu.VMEM((14 * 12, 128), f32),
+            dma((10,)), dma((5,)), dma((7,)), dma((4,)), dma((4,)), dma((2,)), dma((2,)), dma((4,)),
         ],
         compiler_params=pltpu.CompilerParams(
             collective_id=0, has_side_effects=True, vmem_limit_bytes=60 * 1024 * 1024

time: 51.6 us -> 54.8 us (1.062); the launches traced: 50.6 us -> 54.7 us
  Pallas kernels: 48.1 us -> 52.1 us
    pallas_call x1, Pallas kernels: 48.1 us -> 52.1 us  [body(): pl.pallas_call(kernel, out_shape=(out, out), in_specs=[hbm] * 10, out_spe...]
where the time goes in v4:
time: 54.8 us; the launch traced here: 54.7 us
  Pallas kernels  52.1 us (95%)
  between operations  1.29 us (2%)
  local copies, waits for them, and re-layouts  1.28 us (2%)
    pallas_call x1, Pallas kernels, body(): pl.pallas_call(kernel, out_shape=(out, out), in_specs=[hbm] * 10, out_spe...  52.1 us
    unnamed x2, local copies, waits for them, and re-layouts  1.28 us

profile of v4, /device:TPU:1, one launch (start us, length us, event | category | flops | bytes accessed | tf_op | source)
XLA Modules:
  0.0 54.7 jit_solution(7199083859405169965)
XLA Ops:
  1.3 52.1 %fields.1 = (f32[1,3,16,512]{3,2,1,0:T(8,128)S(1)}, f32[1,3,16,512]{3,2,1,0:T(8,128)S(1)}) custom-call(f32[1,16,512]{2,1,0:T(8,128)} %polar_any.1, f32[1,16,512]{2,1,0:T(8,128)} %azimuth_any.1, f32[1,16,512]{2,1,0:T(8,128)} %saturation_any.1, f32[1,16,512]{2,1,0:T(8,128)} %anisotropy_any.1, f32[1]{0:T(128)S(6)} %copy.16.stiffness_any, f32[15]{0:T(128)} %coupling_any.1, ...), custom_call_target="tpu_custom_call" | custom-call | flops 1000000000 | bytes 5000000 | tf_op jit(solution)/shard_map/fields/pallas_call | solution.py:541
  53.4 0.6 %copy.14 = f32[1,3,16,512]{3,2,1,0:T(8,128)} copy(f32[1,3,16,512]{3,2,1,0:T(8,128)S(1)} %get-tuple-element.2) | data formatting | bytes 196608
  54.0 0.6 %copy.15 = f32[1,3,16,512]{3,2,1,0:T(8,128)} copy(f32[1,3,16,512]{3,2,1,0:T(8,128)S(1)} %get-tuple-element.3) | data formatting | bytes 196608

commit v5 on v3

--- a/solution.py
+++ b/solution.py
@@ -227,7 +227,7 @@
             zs[at(1, t, v), :] = uy * h - lone_y * lone
 
 
-def return_x(zs, wxh, wxl, s3):
+def field_rows(zs):
     rows = []
     for c in range(3):
         order = ORDER_X if c == 0 else ORDER
@@ -237,12 +237,15 @@
                     zs[pl.ds(tile_row(c, tg, order.index((a, b)), lb), 8), :] for a in range(2) for lb in range(4)
                 ]
                 rows.append(jnp.concatenate(lanes, 1))
-    out = product(jnp.concatenate(rows, 0), wxh[...], wxl[...], True)
-    for x_lo in range(2):
-        for h in range(2):
-            lane = (x_lo * 2 + h) * 128
-            for q in range(6):
-                s3[pl.ds(x_lo * 12 + h * 6 + q, 16, stride=24), :] = out[16 * q : 16 * q + 16, lane : lane + 128]
+    return jnp.concatenate(rows, 0)
+
+
+def return_x(x_lo, left, wxh, wxl, s3):
+    wanted = pl.ds(pl.multiple_of(x_lo * 256, 256), 256)
+    out = product(left, wxh[wanted, :], wxl[wanted, :], True)
+    for h in range(2):
+        for q in range(6):
+            s3[pl.ds(x_lo * 12 + h * 6 + q, 16, stride=24), :] = out[16 * q : 16 * q + 16, h * 128 : h * 128 + 128]
 
 
 def turn_out(k, r3, s4):
@@ -320,6 +323,36 @@
     source = t * 2 + x_lo
     owner = core * 16 + lax.div(t, 2) * 2 + x_lo
 
+    def ring_device(away):
+        there = lax.rem(z + away, RING)
+        return there, (t, x_lo * RING + there)
+
+    def slab_device(far, there_core):
+        a, b, dy = far
+        there_x = lax.rem(x_lo + b, 2)
+        pair = lax.rem(x_hi + a, 2) * 4 + lax.rem(y + dy, 4)
+        there_t = pair * 2 + there_core
+        return there_t * 2 + there_x, there_core * 16 + pair * 2 + there_x, (there_t, there_x * RING + z)
+
+    next_plane = (t, lax.rem(p + 1, 2 * RING))
+    last_plane = (t, lax.rem(p + 2 * RING - 1, 2 * RING))
+    next_layer = (lax.rem(t + 1, LAYERS), p)
+    last_layer = (lax.rem(t + LAYERS - 1, LAYERS), p)
+
+    barrier = pltpu.get_barrier_semaphore()
+
+    def greet(there):
+        pl.semaphore_signal(barrier, inc=1, device_id=there, device_id_type=MESH)
+
+    for away in AWAY:
+        greet(ring_device(away)[1])
+    for far in FAR:
+        greet(slab_device(far, 1 - core)[2])
+        if any(far):
+            greet(slab_device(far, core)[2])
+    for there in (next_plane, last_plane):
+        greet(there)
+
     loads = [
         pltpu.make_async_copy(src, dst, load_sem.at[i])
         for i, (src, dst) in enumerate([
@@ -330,36 +363,6 @@
     ]
     for load in loads:
         load.start()
-
-    def ring_device(away):
-        there = lax.rem(z + away, RING)
-        return there, (t, x_lo * RING + there)
-
-    def slab_device(far, there_core):
-        a, b, dy = far
-        there_x = lax.rem(x_lo + b, 2)
-        pair = lax.rem(x_hi + a, 2) * 4 + lax.rem(y + dy, 4)
-        there_t = pair * 2 + there_core
-        return there_t * 2 + there_x, there_core * 16 + pair * 2 + there_x, (there_t, there_x * RING + z)
-
-    next_plane = (t, lax.rem(p + 1, 2 * RING))
-    last_plane = (t, lax.rem(p + 2 * RING - 1, 2 * RING))
-    next_layer = (lax.rem(t + 1, LAYERS), p)
-    last_layer = (lax.rem(t + LAYERS - 1, LAYERS), p)
-
-    barrier = pltpu.get_barrier_semaphore()
-
-    def greet(there):
-        pl.semaphore_signal(barrier, inc=1, device_id=there, device_id_type=MESH)
-
-    for away in AWAY:
-        greet(ring_device(away)[1])
-    for far in FAR:
-        greet(slab_device(far, 1 - core)[2])
-        if any(far):
-            greet(slab_device(far, core)[2])
-    for there in (next_plane, last_plane):
-        greet(there)
 
     loads[0].wait()
     loads[1].wait()
@@ -406,14 +409,15 @@
                 def _():
                     remote(rows_of(s2, there), rows_of(r2, source), sems, device).start()
 
-    def slab_return():
+    def slab_return(other):
         sems = (send_sem.at[2], recv_sem.at[3 + core])
-        for far in FAR:
+        for far in [far for far in FAR if far[1] == other]:
             for there_core in (core, 1 - core):
                 there, _, device = slab_device(far, there_core)
                 if any(far) or there_core is not core:
                     remote(rows_of(s3, there), rows_of(r3, owner), sems, device).start()
-        pltpu.make_async_copy(rows_of(s3, source), rows_of(r3, owner), recv_sem.at[3 + core]).start()
+        if not other:
+            pltpu.make_async_copy(rows_of(s3, source), rows_of(r3, owner), recv_sem.at[3 + core]).start()
 
     def received(dst, n, rows=192):
         part = dst.at[pl.ds(0, rows)]
@@ -466,8 +470,10 @@
     received(r2, 2, 384)
     transform_x(r2, wxh, wxl, zs)
     couple(zs, tb, ws)
-    return_x(zs, wxh, wxl, s3)
-    slab_return()
+    left = field_rows(zs)
+    for other in range(2):
+        return_x(lax.rem(x_lo + other, 2), left, wxh, wxl, s3)
+        slab_return(other)
     for k in range(2):
         received(r3, 3 + k)
         turn_out(k, r3, s4)

time: 51.6 us -> 52.9 us (1.025); the launches traced: 50.6 us -> 52.8 us
  Pallas kernels: 48.1 us -> 50.2 us
    pallas_call x1, Pallas kernels: 48.1 us -> 50.2 us  [body(): pl.pallas_call(kernel, out_shape=(out, out), in_specs=[hbm] * 10, out_spe...]
where the time goes in v5:
time: 52.9 us; the launch traced here: 52.8 us
  Pallas kernels  50.2 us (95%)
  between operations  1.29 us (2%)
  local copies, waits for them, and re-layouts  1.28 us (2%)
    pallas_call x1, Pallas kernels, body(): pl.pallas_call(kernel, out_shape=(out, out), in_specs=[hbm] * 10, out_spe...  50.2 us
    unnamed x2, local copies, waits for them, and re-layouts  1.28 us

profile of v5, /device:TPU:1, one launch (start us, length us, event | category | flops | bytes accessed | tf_op | source)
XLA Modules:
  0.0 52.8 jit_solution(11332566564398387261)
XLA Ops:
  1.3 50.2 %fields.1 = (f32[1,3,16,512]{3,2,1,0:T(8,128)S(1)}, f32[1,3,16,512]{3,2,1,0:T(8,128)S(1)}) custom-call(f32[1,16,512]{2,1,0:T(8,128)} %polar_any.1, f32[1,16,512]{2,1,0:T(8,128)} %azimuth_any.1, f32[1,16,512]{2,1,0:T(8,128)} %saturation_any.1, f32[1,16,512]{2,1,0:T(8,128)} %anisotropy_any.1, f32[1]{0:T(128)S(6)} %copy.16.stiffness_any, f32[15]{0:T(128)} %coupling_any.1, ...), custom_call_target="tpu_custom_call" | custom-call | flops 1000000000 | bytes 5000000 | tf_op jit(solution)/shard_map/fields/pallas_call | solution.py:508
  51.5 0.6 %copy.14 = f32[1,3,16,512]{3,2,1,0:T(8,128)} copy(f32[1,3,16,512]{3,2,1,0:T(8,128)S(1)} %get-tuple-element.2) | data formatting | bytes 196608
  52.2 0.6 %copy.15 = f32[1,3,16,512]{3,2,1,0:T(8,128)} copy(f32[1,3,16,512]{3,2,1,0:T(8,128)S(1)} %get-tuple-element.3) | data formatting | bytes 196608

commit v6 on v3

--- a/solution.py
+++ b/solution.py
@@ -320,6 +320,36 @@
     source = t * 2 + x_lo
     owner = core * 16 + lax.div(t, 2) * 2 + x_lo
 
+    def ring_device(away):
+        there = lax.rem(z + away, RING)
+        return there, (t, x_lo * RING + there)
+
+    def slab_device(far, there_core):
+        a, b, dy = far
+        there_x = lax.rem(x_lo + b, 2)
+        pair = lax.rem(x_hi + a, 2) * 4 + lax.rem(y + dy, 4)
+        there_t = pair * 2 + there_core
+        return there_t * 2 + there_x, there_core * 16 + pair * 2 + there_x, (there_t, there_x * RING + z)
+
+    next_plane = (t, lax.rem(p + 1, 2 * RING))
+    last_plane = (t, lax.rem(p + 2 * RING - 1, 2 * RING))
+    next_layer = (lax.rem(t + 1, LAYERS), p)
+    last_layer = (lax.rem(t + LAYERS - 1, LAYERS), p)
+
+    barrier = pltpu.get_barrier_semaphore()
+
+    def greet(there):
+        pl.semaphore_signal(barrier, inc=1, device_id=there, device_id_type=MESH)
+
+    for away in AWAY:
+        greet(ring_device(away)[1])
+    for far in FAR:
+        greet(slab_device(far, 1 - core)[2])
+        if any(far):
+            greet(slab_device(far, core)[2])
+    for there in (next_plane, last_plane):
+        greet(there)
+
     loads = [
         pltpu.make_async_copy(src, dst, load_sem.at[i])
         for i, (src, dst) in enumerate([
@@ -330,36 +360,6 @@
     ]
     for load in loads:
         load.start()
-
-    def ring_device(away):
-        there = lax.rem(z + away, RING)
-        return there, (t, x_lo * RING + there)
-
-    def slab_device(far, there_core):
-        a, b, dy = far
-        there_x = lax.rem(x_lo + b, 2)
-        pair = lax.rem(x_hi + a, 2) * 4 + lax.rem(y + dy, 4)
-        there_t = pair * 2 + there_core
-        return there_t * 2 + there_x, there_core * 16 + pair * 2 + there_x, (there_t, there_x * RING + z)
-
-    next_plane = (t, lax.rem(p + 1, 2 * RING))
-    last_plane = (t, lax.rem(p + 2 * RING - 1, 2 * RING))
-    next_layer = (lax.rem(t + 1, LAYERS), p)
-    last_layer = (lax.rem(t + LAYERS - 1, LAYERS), p)
-
-    barrier = pltpu.get_barrier_semaphore()
-
-    def greet(there):
-        pl.semaphore_signal(barrier, inc=1, device_id=there, device_id_type=MESH)
-
-    for away in AWAY:
-        greet(ring_device(away)[1])
-    for far in FAR:
-        greet(slab_device(far, 1 - core)[2])
-        if any(far):
-            greet(slab_device(far, core)[2])
-    for there in (next_plane, last_plane):
-        greet(there)
 
     loads[0].wait()
     loads[1].wait()
@@ -409,7 +409,7 @@
     def slab_return():
         sems = (send_sem.at[2], recv_sem.at[3 + core])
         for far in FAR:
-            for there_core in (core, 1 - core):
+            for there_core in (1 - core, core):
                 there, _, device = slab_device(far, there_core)
                 if any(far) or there_core is not core:
                     remote(rows_of(s3, there), rows_of(r3, owner), sems, device).start()

time: 51.6 us -> 51.6 us (level)
  the two profiles are of different devices: /device:TPU:1 before, /device:TPU:8 now
where the time goes in v6:
time: 51.6 us; the launch traced here: 51.5 us
  Pallas kernels  48.9 us (95%)
  between operations  1.29 us (2%)
  local copies, waits for them, and re-layouts  1.28 us (2%)
    pallas_call x1, Pallas kernels, body(): pl.pallas_call(kernel, out_shape=(out, out), in_specs=[hbm] * 10, out_spe...  48.9 us
    unnamed x2, local copies, waits for them, and re-layouts  1.28 us

profile of v6, /device:TPU:8, one launch (start us, length us, event | category | flops | bytes accessed | tf_op | source)
XLA Modules:
  0.0 51.5 jit_solution(6729924352787635178)
XLA Ops:
  1.3 48.9 %fields.1 = (f32[1,3,16,512]{3,2,1,0:T(8,128)S(1)}, f32[1,3,16,512]{3,2,1,0:T(8,128)S(1)}) custom-call(f32[1,16,512]{2,1,0:T(8,128)} %polar_any.1, f32[1,16,512]{2,1,0:T(8,128)} %azimuth_any.1, f32[1,16,512]{2,1,0:T(8,128)} %saturation_any.1, f32[1,16,512]{2,1,0:T(8,128)} %anisotropy_any.1, f32[1]{0:T(128)S(6)} %copy.16.stiffness_any, f32[15]{0:T(128)} %coupling_any.1, ...), custom_call_target="tpu_custom_call" | custom-call | flops 1000000000 | bytes 5000000 | tf_op jit(solution)/shard_map/fields/pallas_call | solution.py:502
  50.2 0.6 %copy.14 = f32[1,3,16,512]{3,2,1,0:T(8,128)} copy(f32[1,3,16,512]{3,2,1,0:T(8,128)S(1)} %get-tuple-element.2) | data formatting | bytes 196608
  50.8 0.6 %copy.15 = f32[1,3,16,512]{3,2,1,0:T(8,128)} copy(f32[1,3,16,512]{3,2,1,0:T(8,128)S(1)} %get-tuple-element.3) | data formatting | bytes 196608

commit v7 on v6

--- a/solution.py
+++ b/solution.py
@@ -50,7 +50,7 @@
     sine = np.sin(angle)
     sine[:, 0] = np.where(x % 2 == 0, 1.0, -1.0)
     along_x = np.concatenate([np.cos(angle), sine], 1)
-    return halves(along_y) + halves(along_x)
+    return sum((halves(table) for table in (along_y, along_x, along_x.T, along_y.T)), ())
 
 
 def polynomial(x, coefficients):
@@ -76,11 +76,11 @@
     return sin_p * (1.0 - 2.0 * s * s), sin_p * (2.0 * s * c), cos_p
 
 
-def product(left, high, low, transposed):
+def product(left, high, low):
     left_high = left.astype(bf16)
     left_low = (left - left_high.astype(f32)).astype(bf16)
     rows = left.shape[0]
-    dims = (((1,), (1 if transposed else 0,)), ((), ()))
+    dims = (((1,), (0,)), ((), ()))
     both = lax.dot_general(
         jnp.concatenate([left_high, left_low], 0), high, dims, preferred_element_type=f32
     )
@@ -102,7 +102,7 @@
 
 def forward_y(m, saturation, wyh, wyl, s1):
     rows = [m[c][8 * h : 8 * h + 8] * saturation[8 * h : 8 * h + 8] for h in range(2) for c in range(3)]
-    y = product(jnp.concatenate(rows, 0), wyh[...], wyl[...], False)
+    y = product(jnp.concatenate(rows, 0), wyh[...], wyl[...])
     even, low = even_lanes(), low_lanes(8)
     for c in range(3):
         for p in range(8):
@@ -172,7 +172,7 @@
         for h in range(2):
             parts = [r2[pl.ds(x_lo * 12 + h * 6 + q, 16, stride=24), :] for q in range(6)]
             columns.append(jnp.concatenate(parts, 0))
-    z = product(jnp.concatenate(columns, 1), wxh[...], wxl[...], False)
+    z = product(jnp.concatenate(columns, 1), wxh[...], wxl[...])
     for c in range(3):
         for cls, (a, b) in enumerate(ORDER_X if c == 0 else ORDER):
             for tg in range(2):
@@ -227,7 +227,7 @@
             zs[at(1, t, v), :] = uy * h - lone_y * lone
 
 
-def return_x(zs, wxh, wxl, s3):
+def return_x(zs, xwh, xwl, s3):
     rows = []
     for c in range(3):
         order = ORDER_X if c == 0 else ORDER
@@ -237,7 +237,7 @@
                     zs[pl.ds(tile_row(c, tg, order.index((a, b)), lb), 8), :] for a in range(2) for lb in range(4)
                 ]
                 rows.append(jnp.concatenate(lanes, 1))
-    out = product(jnp.concatenate(rows, 0), wxh[...], wxl[...], True)
+    out = product(jnp.concatenate(rows, 0), xwh[...], xwl[...])
     for x_lo in range(2):
         for h in range(2):
             lane = (x_lo * 2 + h) * 128
@@ -255,7 +255,7 @@
             s4[pl.ds(k * 192 + c * 4 + r, 16, stride=12), :] = block[16 * r : 16 * r + 16]
 
 
-def inverse_y(k, r4, wyh, wyl):
+def inverse_y(k, r4, ywh, ywl):
     even = even_lanes()
     kept = low_lanes(8) == (lax.broadcasted_iota(jnp.int32, (8, 128), 0) < 4)
 
@@ -273,8 +273,8 @@
             low.append(jnp.where(even, pltpu.roll(first, 127, 1), second))
         upper.append(jnp.concatenate(up, 1))
         lower.append(jnp.concatenate(low, 1))
-    columns = slice(512 * k, 512 * k + 512)
-    return product(jnp.concatenate(upper + lower, 0), wyh[:, columns], wyl[:, columns], True)
+    wanted = slice(512 * k, 512 * k + 512)
+    return product(jnp.concatenate(upper + lower, 0), ywh[wanted], ywl[wanted])
 
 
 def cross_product(a, b):
@@ -304,10 +304,10 @@
 
 def kernel(
     polar_any, azimuth_any, saturation_any, anisotropy_any, stiffness_any, coupling_any,
-    wyh_any, wyl_any, wxh_any, wxl_any,
+    wyh_any, wyl_any, wxh_any, wxl_any, xwh_any, xwl_any, ywh_any, ywl_any,
     field_out, moment_out,
     polar, azimuth, saturation, anisotropy, stiffness, coupling,
-    wyh, wyl, wxh, wxl, s1, r1, s2, r2, s3, r3, s4, r4, zs, ws, tb, near, edge_out, edge_in, rest,
+    wyh, wyl, wxh, wxl, xwh, xwl, ywh, ywl, s1, r1, s2, r2, s3, r3, s4, r4, zs, ws, tb, near, edge_out, edge_in, rest,
     load_sem, send_sem, recv_sem, near_send, near_recv, edge_send, edge_recv,
 ):
     t = lax.axis_index("layer")
@@ -355,7 +355,7 @@
         for i, (src, dst) in enumerate([
             (polar_any, polar), (azimuth_any, azimuth), (saturation_any, saturation), (wyh_any, wyh), (wyl_any, wyl),
             (anisotropy_any, anisotropy), (stiffness_any, stiffness), (coupling_any, coupling),
-            (wxh_any, wxh), (wxl_any, wxl),
+            (wxh_any, wxh), (wxl_any, wxl), (xwh_any, xwh), (xwl_any, xwl), (ywh_any, ywh), (ywl_any, ywl),
         ])
     ]
     for load in loads:
@@ -466,16 +466,16 @@
     received(r2, 2, 384)
     transform_x(r2, wxh, wxl, zs)
     couple(zs, tb, ws)
-    return_x(zs, wxh, wxl, s3)
+    return_x(zs, xwh, xwl, s3)
     slab_return()
     for k in range(2):
         received(r3, 3 + k)
         turn_out(k, r3, s4)
         ring_send(s4, r4, 3, k, 5 + k)
     received(r4, 5)
-    demag = inverse_y(0, r4, wyh, wyl)
+    demag = inverse_y(0, r4, ywh, ywl)
     received(r4, 6)
-    demag = demag + inverse_y(1, r4, wyh, wyl)
+    demag = demag + inverse_y(1, r4, ywh, ywl)
     m = [rest[3 + c] for c in range(3)]
     field = [
         jnp.concatenate([demag[8 * c : 8 * c + 8], demag[24 + 8 * c : 32 + 8 * c]], 0) + rest[c] for c in range(3)
@@ -497,20 +497,18 @@
     hbm = pl.BlockSpec(memory_space=pltpu.HBM)
     out = pltpu.VMEM((1, 3, 16, CELLS), f32)
     dma = pltpu.SemaphoreType.DMA
+    table, turned = pltpu.VMEM((CELLS, PAD), bf16), pltpu.VMEM((PAD, CELLS), bf16)
     block = pltpu.VMEM((SLAB * 12, 128), f32)
     row_block = pltpu.VMEM((1, 16, CELLS), f32)
     return pl.pallas_call(
         kernel,
         out_shape=(out, out),
-        in_specs=[hbm] * 10,
+        in_specs=[hbm] * 14,
         out_specs=(vmem, vmem),
         scratch_shapes=[
             row_block, row_block, row_block, row_block,
             pltpu.SMEM((1,), f32), pltpu.SMEM((LAYERS - 1,), f32),
-            pltpu.VMEM((CELLS, PAD), bf16),
-            pltpu.VMEM((CELLS, PAD), bf16),
-            pltpu.VMEM((CELLS, PAD), bf16),
-            pltpu.VMEM((CELLS, PAD), bf16),
+            table, table, table, table, turned, turned, turned, turned,
             block, block, block, block, block, block, block, block,
             pltpu.VMEM((3 * 2 * 16 * 8, 128), f32),
             pltpu.VMEM((2, LAYERS, 4, 8, 128), f32),
@@ -519,7 +517,7 @@
             pltpu.VMEM((2, 16, 128), f32),
             pltpu.VMEM((2, 16, 128), f32),
             pltpu.VMEM((6, 16, CELLS), f32),
-            dma((10,)), dma((4,)), dma((7,)), dma((4,)), dma((4,)), dma((2,)), dma((2,)),
+            dma((14,)), dma((4,)), dma((7,)), dma((4,)), dma((4,)), dma((2,)), dma((2,)),
         ],
         compiler_params=pltpu.CompilerParams(
             collective_id=0, has_side_effects=True, vmem_limit_bytes=60 * 1024 * 1024

time: 51.6 us -> 51.3 us (level)
  no operation moved by 1% of the time
where the time goes in v7:
time: 51.3 us; the launch traced here: 51.1 us
  Pallas kernels  48.6 us (95%)
  between operations  1.29 us (3%)
  local copies, waits for them, and re-layouts  1.28 us (2%)
    pallas_call x1, Pallas kernels, body(): pl.pallas_call(kernel, out_shape=(out, out), in_specs=[hbm] * 14, out_spe...  48.6 us
    unnamed x2, local copies, waits for them, and re-layouts  1.28 us

profile of v7, /device:TPU:8, one launch (start us, length us, event | category | flops | bytes accessed | tf_op | source)
XLA Modules:
  0.0 51.1 jit_solution(14671643225047564954)
XLA Ops:
  1.3 48.6 %fields.1 = (f32[1,3,16,512]{3,2,1,0:T(8,128)S(1)}, f32[1,3,16,512]{3,2,1,0:T(8,128)S(1)}) custom-call(f32[1,16,512]{2,1,0:T(8,128)} %polar_any.1, f32[1,16,512]{2,1,0:T(8,128)} %azimuth_any.1, f32[1,16,512]{2,1,0:T(8,128)} %saturation_any.1, f32[1,16,512]{2,1,0:T(8,128)} %anisotropy_any.1, f32[1]{0:T(128)S(6)} %copy.20.stiffness_any, f32[15]{0:T(128)} %coupling_any.1, ...), custom_call_target="tpu_custom_call" | custom-call | flops 1000000000 | bytes 5000000 | tf_op jit(solution)/shard_map/fields/pallas_call | solution.py:503
  49.8 0.6 %copy.18 = f32[1,3,16,512]{3,2,1,0:T(8,128)} copy(f32[1,3,16,512]{3,2,1,0:T(8,128)S(1)} %get-tuple-element.2) | data formatting | bytes 196608
  50.5 0.6 %copy.19 = f32[1,3,16,512]{3,2,1,0:T(8,128)} copy(f32[1,3,16,512]{3,2,1,0:T(8,128)S(1)} %get-tuple-element.3) | data formatting | bytes 196608
